TPU v7x, 32 devices: a whole 2x2x4 slice. The times are simulated.
32 devices in a mesh: groups: 2 (over y), ctx: 16 (over z, x, core).
Axes of the slice: x: 2, y: 2, z: 4, core: 2. Of those that a mesh axis runs over, the one named last changes fastest.
Arguments:
- hidden_in: bfloat16 [4096, 8192], P(('groups', 'ctx')), parts along dimension 0, may hold values from -6 to 6
- queries: bfloat16 [4096, 4096], P(('groups', 'ctx')), parts along dimension 0, may hold values from -5 to 5
- keys: bfloat16 [4096, 512], P(('groups', 'ctx')), parts along dimension 0, may hold values from -5 to 5
- frozen_values: bfloat16 [4096, 512], P(('groups', 'ctx')), parts along dimension 0, may hold values from -6 to 6
- d_out: bfloat16 [4096, 4096], P(('groups', 'ctx')), parts along dimension 0, may hold values from -1.5 to 1.5
- adapter_down: bfloat16 [16, 8192, 16], P(None, 'ctx'), may hold values from -0.0625 to 0.0625
- adapter_up: bfloat16 [16, 8192], P(None, 'ctx'), may hold values from -0.29882812 to 0.29882812
- seg_tiles: int32 [16], P('groups'), parts along dimension 0, may hold values from 1 to 4, as said below
- seg_tenant: int32 [16], P('groups'), parts along dimension 0, may hold values from 0 to 15
Outputs:
- d_queries: bfloat16 [4096, 4096], P(('groups', 'ctx')), parts along dimension 0
- d_keys: bfloat16 [4096, 512], P(('groups', 'ctx')), parts along dimension 0
- d_values: bfloat16 [4096, 512], P(('groups', 'ctx')), parts along dimension 0
- d_adapter_down: float32 [32, 8192, 16], P('groups', 'ctx'), parts along dimension 0
- d_adapter_up: float32 [32, 8192], P('groups', 'ctx'), parts along dimension 0
There are 2 independent parts, one for each index of `groups`. A program takes and returns all parts, laid end to end along the dimension named above; an argument that names none is the same for every part. Nothing has to cross between parts.
Inputs may be any that keep to these rules, and one draw needn't show every extreme that they name: Segment i covers seg_tiles[i] whole tiles of 128 rows; together they cover all 16 tiles, and some segment has exactly 4 tiles.
All inputs are finite; a program needn't handle non-finite values.
Results may differ from a plain program's by a relative error of at most 0.011.
Values may be sent and summed in bfloat16 or wider, within the bound.
A program may use at most 128 MiB of HBM per device.

v0:
```python
import jax
import jax.numpy as jnp
from jax import lax
from jax.sharding import PartitionSpec as P

D = 8192
QUERY_HEADS = 32
KEY_VALUE_HEADS = 4
HEAD_SIZE = 128
R = 16
TILE = 128
SEGMAX = 512


ADAPTER_SCALE = 2.0
NEG_BIG = -1e30


def shifted(array, axis, by):
    length = lax.axis_size(axis)
    pairs = [(i, i + by) for i in range(length) if 0 <= i + by < length]
    return lax.ppermute(array, axis, pairs)


def tile_segments(seg_tiles, total_tiles):
    segment_ends = jnp.cumsum(seg_tiles)
    tile_index = jnp.arange(total_tiles, dtype=jnp.int32)
    return jnp.sum((segment_ends[None, :] <= tile_index[:, None]).astype(jnp.int32), axis=1)


def window_grads(rows_of_query, rows_of_key, rows_of_value, gradient_rows, allowed):
    count_of_query = rows_of_query.shape[0]
    window_length = rows_of_key.shape[0]
    group_width = QUERY_HEADS // KEY_VALUE_HEADS
    score_scale = 1.0 / jnp.sqrt(jnp.float32(HEAD_SIZE))
    heads_of_query = rows_of_query.reshape(count_of_query, KEY_VALUE_HEADS, group_width, HEAD_SIZE)
    gradient_heads = gradient_rows.reshape(count_of_query, KEY_VALUE_HEADS, group_width, HEAD_SIZE)
    heads_of_key = rows_of_key.reshape(window_length, KEY_VALUE_HEADS, HEAD_SIZE)
    heads_of_value = rows_of_value.reshape(window_length, KEY_VALUE_HEADS, HEAD_SIZE)
    query_list = []
    key_collection = []
    value_collection = []
    for key_value_head in range(KEY_VALUE_HEADS):
        query_part = heads_of_query[:, key_value_head]
        grad_part = gradient_heads[:, key_value_head]
        key_part = heads_of_key[:, key_value_head]
        value_part = heads_of_value[:, key_value_head]
        scores = (
            jnp.einsum("tgd,wd->gtw", query_part, key_part, preferred_element_type=jnp.float32)
            * score_scale
        )
        scores = jnp.where(allowed[None], scores, NEG_BIG)
        row_top = jnp.max(scores, axis=-1, keepdims=True)
        weights = jnp.where(allowed[None], jnp.exp(scores - row_top), 0.0)
        prob_full = weights / jnp.sum(weights, axis=-1, keepdims=True)
        prob_half = prob_full.astype(jnp.bfloat16)
        attended = jnp.einsum(
            "gtw,wd->tgd", prob_half, value_part, preferred_element_type=jnp.float32
        ).astype(jnp.bfloat16)
        attended = lax.optimization_barrier(attended)
        row_delta = jnp.sum(grad_part.astype(jnp.float32) * attended.astype(jnp.float32), axis=-1).T
        d_prob = jnp.einsum(
            "tgd,wd->gtw", grad_part, value_part, preferred_element_type=jnp.float32
        )
        d_score = (prob_full * (d_prob - row_delta[:, :, None]) * score_scale).astype(jnp.bfloat16)
        query_list.append(
            jnp.einsum("gtw,wd->tgd", d_score, key_part, preferred_element_type=jnp.float32)
        )
        key_collection.append(
            jnp.einsum("gtw,tgd->wd", d_score, query_part, preferred_element_type=jnp.float32)
        )
        value_collection.append(
            jnp.einsum("gtw,tgd->wd", prob_half, grad_part, preferred_element_type=jnp.float32)
        )
    d_query = jnp.stack(query_list, axis=1).reshape(count_of_query, QUERY_HEADS * HEAD_SIZE)
    key_gradient = jnp.stack(key_collection, axis=1).reshape(
        window_length, KEY_VALUE_HEADS * HEAD_SIZE
    )
    value_gradient = jnp.stack(value_collection, axis=1).reshape(
        window_length, KEY_VALUE_HEADS * HEAD_SIZE
    )
    return (d_query, key_gradient, value_gradient)


def per_device(
    hidden_in, queries, keys, frozen_values, d_out, adapter_down, adapter_up, seg_tiles, seg_tenant
):
    devices = lax.axis_size("ctx")
    position = lax.axis_index("ctx")
    row_count = queries.shape[0]
    slot_count = row_count // TILE
    adapter_count = adapter_down.shape[0]
    key_value_width = keys.shape[1]
    total_tiles = row_count * devices // TILE
    reach = (SEGMAX - TILE + row_count - 1) // row_count
    tile_segment = tile_segments(seg_tiles, total_tiles)
    tenant_per_tile = jnp.take(seg_tenant, tile_segment)
    slot_order = tenant_per_tile.reshape(devices, slot_count).T.reshape(-1)
    down_rows = adapter_down.reshape(adapter_count, -1)
    send_down = jnp.take(down_rows, slot_order, axis=0).reshape(slot_count, devices, -1)
    send_up = jnp.take(adapter_up, slot_order, axis=0).reshape(slot_count, devices, -1)
    recv_down, recv_up = (
        lax.all_to_all(send_down, "ctx", split_axis=1, concat_axis=1, tiled=True),
        lax.all_to_all(send_up, "ctx", split_axis=1, concat_axis=1, tiled=True),
    )
    down_mats = recv_down.reshape(slot_count, D, R)
    up_mats = recv_up.reshape(slot_count, R, key_value_width)
    input_tiles = hidden_in.reshape(slot_count, TILE, D)
    low_rank_product = jnp.einsum(
        "ktd,kdr->ktr", input_tiles, down_mats, preferred_element_type=jnp.float32
    ).astype(jnp.bfloat16)
    adapter_term = jnp.einsum(
        "mqw,mws->mqs", low_rank_product, up_mats, preferred_element_type=jnp.float32
    ).reshape(row_count, key_value_width)
    value_matrix = (frozen_values.astype(jnp.float32) + ADAPTER_SCALE * adapter_term).astype(
        jnp.bfloat16
    )
    key_pieces = [keys]
    value_pieces = [value_matrix]
    for distance in range(1, reach + 1):
        far_keys, far_values = shifted((keys, value_matrix), "ctx", distance)
        key_pieces.insert(0, far_keys)
        value_pieces.insert(0, far_values)
    window_keys = jnp.concatenate(key_pieces, axis=0)
    window_values = jnp.concatenate(value_pieces, axis=0)
    padded_segment = jnp.concatenate(
        [jnp.full((reach * slot_count,), -1, jnp.int32), tile_segment], axis=0
    )
    window_tiles = lax.dynamic_slice_in_dim(
        padded_segment, position * slot_count, (reach + 1) * slot_count, 0
    )
    window_segment = jnp.repeat(window_tiles, TILE)
    query_segment = window_segment[-row_count:]
    window_length = window_segment.shape[0]
    key_place = jnp.arange(window_length, dtype=jnp.int32)
    query_place = reach * row_count + jnp.arange(row_count, dtype=jnp.int32)
    allowed = (query_segment[:, None] == window_segment[None, :]) & (
        key_place[None, :] <= query_place[:, None]
    )
    d_query, key_gradient, value_gradient = window_grads(
        queries, window_keys, window_values, d_out, allowed
    )
    own_key = key_gradient[-row_count:]
    own_value = value_gradient[-row_count:]
    for distance in range(reach, 0, -1):
        offset = (reach - distance) * row_count
        back_key, back_value = shifted(
            (
                key_gradient[offset : offset + row_count],
                value_gradient[offset : offset + row_count],
            ),
            "ctx",
            -distance,
        )
        own_key = own_key + back_key
        own_value = own_value + back_value
    d_queries = d_query.astype(jnp.bfloat16)
    d_keys = own_key.astype(jnp.bfloat16)
    d_values = own_value.astype(jnp.bfloat16)
    tiles_of_value = d_values.reshape(slot_count, TILE, key_value_width)
    low_rank_gradient = (
        ADAPTER_SCALE
        * jnp.einsum("ihx,idx->ihd", tiles_of_value, up_mats, preferred_element_type=jnp.float32)
    ).astype(jnp.bfloat16)
    up_gradient = ADAPTER_SCALE * jnp.einsum(
        "wmh,wmi->whi", low_rank_product, tiles_of_value, preferred_element_type=jnp.float32
    )
    down_grad = jnp.einsum(
        "ktd,ktr->kdr", input_tiles, low_rank_gradient, preferred_element_type=jnp.float32
    )
    recv_down_grad, recv_up_grad = (
        lax.all_to_all(
            down_grad.reshape(slot_count, devices, -1),
            "ctx",
            split_axis=1,
            concat_axis=1,
            tiled=True,
        ),
        lax.all_to_all(
            up_gradient.reshape(slot_count, devices, -1),
            "ctx",
            split_axis=1,
            concat_axis=1,
            tiled=True,
        ),
    )
    tenant_pick = (
        jnp.arange(adapter_count, dtype=jnp.int32)[:, None] == slot_order[None, :]
    ).astype(jnp.float32)
    d_adapter_down = jnp.dot(
        tenant_pick,
        recv_down_grad.reshape(slot_count * devices, -1),
        precision=lax.Precision.HIGHEST,
        preferred_element_type=jnp.float32,
    ).reshape(adapter_count, -1, R)
    d_adapter_up = jnp.dot(
        tenant_pick,
        recv_up_grad.reshape(slot_count * devices, -1),
        precision=lax.Precision.HIGHEST,
        preferred_element_type=jnp.float32,
    )
    return (d_queries, d_keys, d_values, d_adapter_down, d_adapter_up)


def solution(mesh):
    placed = (
        P(("groups", "ctx"), None),
        P(("groups", "ctx"), None),
        P(("groups", "ctx"), None),
        P(("groups", "ctx"), None),
        P(("groups", "ctx"), None),
        P(None, "ctx", None),
        P(None, "ctx"),
        P("groups"),
        P("groups"),
    )
    return jax.shard_map(
        per_device,
        mesh=mesh,
        in_specs=placed,
        out_specs=(
            P(("groups", "ctx"), None),
            P(("groups", "ctx"), None),
            P(("groups", "ctx"), None),
            P("groups", "ctx", None),
            P("groups", "ctx"),
        ),
        check_vma=False,
    )
```

profile of v0, /device:TPU:1, one launch (start us, length us, event | category | flops | bytes accessed | tf_op | source)
XLA Modules:
  0.0 199.0 jit_solution(7110972156597909416)
XLA Ops:
  1.8 4.5 %collective-permute-start.2 = (bf16[128,512]{0,1:T(8,128)(2,1)S(1)}, bf16[128,512]{0,1:T(8,128)(2,1)}, u32[]{:S(2)}, u32[]{:S(2)}) collective-permute-start(bf16[128,512]{0,1:T(8,128)(2,1)S(1)} %copy.286), channel_id=1, source_target_pairs={{0,1},{1,2},{2,3},{3,4},{4,5},{5,6},{6,7},{7,8},{8,9},{9,10},{10,1... | collective-permute-start | bytes 393224 | tf_op jit(solution)/shard_map/ppermute | solution.py:22
  6.3 3.8 %collective-permute-start.1 = (bf16[128,512]{0,1:T(8,128)(2,1)S(1)}, bf16[128,512]{0,1:T(8,128)(2,1)}, u32[]{:S(2)}, u32[]{:S(2)}) collective-permute-start(bf16[128,512]{0,1:T(8,128)(2,1)S(1)} %copy.286), channel_id=1, source_target_pairs={{0,2},{1,3},{2,4},{3,5},{4,6},{5,7},{6,8},{7,9},{8,10},{9,11},{10,... | collective-permute-start | bytes 393224 | tf_op jit(solution)/shard_map/ppermute | solution.py:22
  18.5 4.6 %all-to-all-start.1 = ((bf16[16,2,256]{2,1,0:T(2,128)(2,1)}), bf16[16,2,256]{2,1,0:T(2,128)(2,1)S(1)}, u32[]{:S(2)}, u32[]{:S(2)}) async-start(bf16[16,2,256]{2,1,0:T(2,128)(2,1)} %reshape.349), calls=%async_computation.1 | async-start | bytes 32768 | tf_op jit(solution)/shard_map/all_to_all | solution.py:104
  31.3 4.7 %reshape.288 = bf16[16,8192]{1,0:T(8,128)(2,1)S(1)} reshape(bf16[16,512,16]{2,1,0:T(8,128)(2,1)} %copy.293) | data formatting | bytes 524288 | tf_op jit(solution)/shard_map/reshape | solution.py:99
  40.3 3.3 %fusion.101 = (f32[8,128]{1,0:T(8,128)S(1)}, f32[8,128,512]{1,2,0:T(8,128)}) fusion(pred[128,512]{0,1:T(8,128)(4,1)S(1)} %fusion.56, bf16[128,4,8,128]{0,3,2,1:T(8,128)(2,1)} %bitcast.389, bf16[512,4,128]{0,2,1:T(8,128)(2,1)} %bitcast.399), kind=kOutput, calls=%fused_computation.181 | convolution fusion | flops 136839680 | bytes 2625536 | tf_op jit(solution)/shard_map/sub | solution.py:54
  43.5 3.3 %fusion.100 = (f32[8,128]{1,0:T(8,128)S(1)}, f32[8,128,512]{1,2,0:T(8,128)}) fusion(pred[128,512]{0,1:T(8,128)(4,1)S(1)} %fusion.56, bf16[128,4,8,128]{0,3,2,1:T(8,128)(2,1)} %bitcast.390, bf16[512,4,128]{0,2,1:T(8,128)(2,1)} %bitcast.400), kind=kOutput, calls=%fused_computation.180 | convolution fusion | flops 136839680 | bytes 2625536 | tf_op jit(solution)/shard_map/sub | solution.py:54
  46.9 3.3 %fusion.99 = (f32[8,128]{1,0:T(8,128)S(1)}, f32[8,128,512]{1,2,0:T(8,128)}) fusion(pred[128,512]{0,1:T(8,128)(4,1)S(1)} %fusion.56, bf16[128,4,8,128]{0,3,2,1:T(8,128)(2,1)} %bitcast.391, bf16[512,4,128]{0,2,1:T(8,128)(2,1)} %bitcast.401), kind=kOutput, calls=%fused_computation.179 | convolution fusion | flops 136839680 | bytes 2625536 | tf_op jit(solution)/shard_map/sub | solution.py:54
  50.2 3.3 %fusion.102 = (f32[8,128]{1,0:T(8,128)S(1)}, f32[8,128,512]{1,2,0:T(8,128)}) fusion(pred[128,512]{0,1:T(8,128)(4,1)S(1)} %fusion.56, bf16[128,4,8,128]{0,3,2,1:T(8,128)(2,1)} %bitcast.392, bf16[512,4,128]{0,2,1:T(8,128)(2,1)} %bitcast.402), kind=kOutput, calls=%fused_computation.182 | convolution fusion | flops 136839680 | bytes 2625536 | tf_op jit(solution)/shard_map/sub | solution.py:54
  84.8 3.2 %reduce.2 = bf16[16,8192]{1,0:T(8,128)(2,1)S(1)} reduce(bf16[16,1,8192]{2,1,0:T(2,128)(2,1)} %bitcast.398, bf16[]{:T(256)} %broadcast.286), dimensions={1}, to_apply=%bitcast.377.reduce_sub_computation | reduce | bytes 524290
  88.9 9.3 %all-to-all-start = ((bf16[16,2,4096]{2,1,0:T(2,128)(2,1)}), bf16[16,2,4096]{2,1,0:T(2,128)(2,1)S(1)}, u32[]{:S(2)}, u32[]{:S(2)}) async-start(bf16[16,2,4096]{2,1,0:T(2,128)(2,1)} %reshape.347), calls=%async_computation | async-start | bytes 524288 | tf_op jit(solution)/shard_map/all_to_all | solution.py:103
  104.1 3.5 %copy.355 = f32[8192,16]{1,0:T(8,128)} copy(f32[8192,16]{0,1:T(8,128)} %convolution_bitcast_fusion) | data formatting | bytes 1048576 | tf_op jit(solution)/shard_map/ktd,ktr->kdr/dot_general | solution.py:168
  107.6 4.2 %reshape.345 = f32[1,16,8192]{2,0,1:T(1,128)} reshape(f32[8192,16]{1,0:T(8,128)} %copy.355) | data formatting | bytes 1048576 | tf_op jit(solution)/shard_map/reshape | solution.py:173
  112.8 2.6 %bitcast_reduce_fusion = bf16[16,8192]{1,0:T(8,128)(2,1)S(1)} fusion(bf16[16,1,8192]{2,1,0:T(2,128)(2,1)} %reshape.348), kind=kLoop, calls=%fused_computation.183 | loop fusion | bytes 524288 | tf_op jit(solution)/shard_map/all_to_all | solution.py:103
  115.4 2.7 %reshape.289 = bf16[8192,16]{1,0:T(8,128)(2,1)} reshape(bf16[16,8192]{1,0:T(8,128)(2,1)S(1)} %bitcast_reduce_fusion) | data formatting | bytes 524288 | tf_op jit(solution)/shard_map/reshape.8
  121.1 6.0 %all-to-all-start.3 = ((f32[1,16,512]{2,0,1:T(1,128)}), f32[1,16,512]{2,0,1:T(1,128)S(1)}, u32[]{:S(2)}, u32[]{:S(2)}) async-start(f32[1,16,512]{2,0,1:T(1,128)} %copy.358), calls=%async_computation.3 | async-start | bytes 65536 | tf_op jit(solution)/shard_map/all_to_all | solution.py:179
  127.4 3.5 %collective-permute-start.5 = (bf16[128,512]{1,0:T(8,128)(2,1)S(1)}, bf16[128,512]{1,0:T(8,128)(2,1)S(1)}, u32[]{:S(2)}, u32[]{:S(2)}) collective-permute-start(bf16[128,512]{1,0:T(8,128)(2,1)S(1)} %fusion.29), channel_id=1, source_target_pairs={{0,1},{1,2},{2,3},{3,4},{4,5},{5,6},{6,7},{7,8},{8,9},{9,10},{10,1... | collective-permute-start | bytes 393224 | tf_op jit(solution)/shard_map/ppermute | solution.py:22
  130.9 3.7 %collective-permute-start.4 = (bf16[128,512]{1,0:T(8,128)(2,1)S(1)}, bf16[128,512]{1,0:T(8,128)(2,1)}, u32[]{:S(2)}, u32[]{:S(2)}) collective-permute-start(bf16[128,512]{1,0:T(8,128)(2,1)S(1)} %fusion.29), channel_id=1, source_target_pairs={{0,2},{1,3},{2,4},{3,5},{4,6},{5,7},{6,8},{7,9},{8,10},{9,11},{10,... | collective-permute-start | bytes 393224 | tf_op jit(solution)/shard_map/ppermute | solution.py:22
  137.0 5.1 %all-to-all-start.2 = ((f32[1,16,8192]{2,0,1:T(1,128)}), f32[1,16,8192]{2,0,1:T(1,128)}, u32[]{:S(2)}, u32[]{:S(2)}) async-start(f32[1,16,8192]{2,0,1:T(1,128)} %reshape.345), calls=%async_computation.2 | async-start | bytes 1048576 | tf_op jit(solution)/shard_map/all_to_all | solution.py:172
  146.7 2.7 %fusion.98 = (bf16[512,1,128]{2,1,0:T(2,128)(2,1)S(1)}, bf16[512,1,128]{2,1,0:T(2,128)(2,1)S(1)}, bf16[512,1,128]{2,1,0:T(2,128)(2,1)S(1)}, bf16[512,1,128]{2,1,0:T(2,128)(2,1)S(1)}) fusion(bf16[512,4,128]{2,1,0:T(4,128)(2,1)} %reshape.291), kind=kLoop, calls=%fused_computation.178 | loop fusion | bytes 1048576 | tf_op jit(solution)/shard_map/slice | solution.py:47
  170.2 2.4 %collective-permute-start.8 = (f32[128,512]{1,0:T(8,128)}, f32[128,512]{1,0:T(8,128)}, u32[]{:S(2)}, u32[]{:S(2)}) collective-permute-start(f32[128,512]{1,0:T(8,128)} %copy.342), channel_id=1, source_target_pairs={{1,0},{2,1},{3,2},{4,3},{5,4},{6,5},{7,6},{8,7},{9,8},{10,9},{11,1... | collective-permute-start | bytes 786440 | tf_op jit(solution)/shard_map/ppermute | solution.py:22
  179.6 5.1 %collective-permute-done.8 = f32[128,512]{1,0:T(8,128)} collective-permute-done((f32[128,512]{1,0:T(8,128)}, f32[128,512]{1,0:T(8,128)}, u32[]{:S(2)}, u32[]{:S(2)}) %collective-permute-start.8) | collective-permute-done | bytes 262176 | tf_op jit(solution)/shard_map/ppermute | solution.py:22
  184.7 3.9 %collective-permute-done.6 = f32[128,512]{1,0:T(8,128)} collective-permute-done((f32[128,512]{1,0:T(8,128)}, f32[128,512]{1,0:T(8,128)}, u32[]{:S(2)}, u32[]{:S(2)}) %collective-permute-start.6) | collective-permute-done | bytes 262176 | tf_op jit(solution)/shard_map/ppermute | solution.py:22
  191.9 2.8 %dot_general.129 = f32[512,16,16]{1,0,2:T(8,128)} reshape(f32[8192,16]{0,1:T(8,128)S(1)} %bitcast.397) | data formatting | bytes 1048576 | tf_op jit(solution)/shard_map/dot_general | solution.py:190
  194.6 2.9 %copy.357 = f32[512,16,16]{0,2,1:T(8,128)S(1)} copy(f32[512,16,16]{1,0,2:T(8,128)} %dot_general.129) | data formatting | bytes 1048576 | tf_op jit(solution)/shard_map/dot_general | solution.py:190
  (200 shorter events, 103.1 us)
Async XLA Ops:
  0.6 101.3 %copy-start = (bf16[128,8192]{1,0:T(8,128)(2,1)S(1)}, bf16[128,8192]{1,0:T(8,128)(2,1)}, u32[]{:S(2)}) copy-start(bf16[128,8192]{1,0:T(8,128)(2,1)} %param.9) | copy-start | bytes 6291460
  1.8 36.5 %collective-permute-start.2 = (bf16[128,512]{0,1:T(8,128)(2,1)S(1)}, bf16[128,512]{0,1:T(8,128)(2,1)}, u32[]{:S(2)}, u32[]{:S(2)}) collective-permute-start(bf16[128,512]{0,1:T(8,128)(2,1)S(1)} %copy.286), channel_id=1, source_target_pairs={{0,1},{1,2},{2,3},{3,4},{4,5},{5,6},{6,7},{7,8},{8,9},{9,10},{10,1... | collective-permute-start | bytes 393224 | tf_op jit(solution)/shard_map/ppermute | solution.py:22
  6.3 32.0 %collective-permute-start.1 = (bf16[128,512]{0,1:T(8,128)(2,1)S(1)}, bf16[128,512]{0,1:T(8,128)(2,1)}, u32[]{:S(2)}, u32[]{:S(2)}) collective-permute-start(bf16[128,512]{0,1:T(8,128)(2,1)S(1)} %copy.286), channel_id=1, source_target_pairs={{0,2},{1,3},{2,4},{3,5},{4,6},{5,7},{6,8},{7,9},{8,10},{9,11},{10,... | collective-permute-start | bytes 393224 | tf_op jit(solution)/shard_map/ppermute | solution.py:22
  10.2 28.2 %collective-permute-start = (bf16[128,512]{0,1:T(8,128)(2,1)S(1)}, bf16[128,512]{0,1:T(8,128)(2,1)}, u32[]{:S(2)}, u32[]{:S(2)}) collective-permute-start(bf16[128,512]{0,1:T(8,128)(2,1)S(1)} %copy.286), channel_id=1, source_target_pairs={{0,3},{1,4},{2,5},{3,6},{4,7},{5,8},{6,9},{7,10},{8,11},{9,12},{10... | collective-permute-start | bytes 393224 | tf_op jit(solution)/shard_map/ppermute | solution.py:22
  18.5 70.3 %all-to-all-start.1 = ((bf16[16,2,256]{2,1,0:T(2,128)(2,1)}), bf16[16,2,256]{2,1,0:T(2,128)(2,1)S(1)}, u32[]{:S(2)}, u32[]{:S(2)}) async-start(bf16[16,2,256]{2,1,0:T(2,128)(2,1)} %reshape.349), calls=%async_computation.1 | async-start | bytes 32768 | tf_op jit(solution)/shard_map/all_to_all | solution.py:104
  29.5 29.0 %copy-start.7 = (bf16[128,4096]{0,1:T(8,128)(2,1)}, bf16[128,4096]{0,1:T(8,128)(2,1)S(1)}, u32[]{:S(2)}) copy-start(bf16[128,4096]{0,1:T(8,128)(2,1)S(1)} %copy.297) | copy-start | bytes 3145732
  43.5 9.9 %copy-start.42 = (f32[8,128]{1,0:T(8,128)}, f32[8,128]{1,0:T(8,128)S(1)}, u32[]{:S(2)}) copy-start(f32[8,128]{1,0:T(8,128)S(1)} %get-tuple-element.52) | copy-start | bytes 12292
  62.0 11.3 %copy-start.22 = (bf16[16,8192]{1,0:T(8,128)(2,1)S(1)}, bf16[16,8192]{1,0:T(8,128)(2,1)}, u32[]{:S(2)}) copy-start(bf16[16,8192]{1,0:T(8,128)(2,1)} %gather_fusion.1) | copy-start | bytes 786436
  62.0 11.3 %copy-start.35 = (pred[16]{0:T(512)(128)(4,1)S(1)}, pred[16]{0:T(512)(128)(4,1)}, u32[]{:S(2)}) copy-start(pred[16]{0:T(512)(128)(4,1)} %copy-done.34) | copy-start | bytes 52
  68.4 32.2 %collective-permute-start.10 = (f32[128,512]{1,0:T(8,128)}, f32[128,512]{1,0:T(8,128)}, u32[]{:S(2)}, u32[]{:S(2)}) collective-permute-start(f32[128,512]{1,0:T(8,128)} %copy.353), channel_id=1, source_target_pairs={{2,0},{3,1},{4,2},{5,3},{6,4},{7,5},{8,6},{9,7},{10,8},{11,9},{12,... | collective-permute-start | bytes 786440 | tf_op jit(solution)/shard_map/ppermute | solution.py:22
  69.7 30.9 %collective-permute-start.11 = (f32[128,512]{1,0:T(8,128)}, f32[128,512]{1,0:T(8,128)}, u32[]{:S(2)}, u32[]{:S(2)}) collective-permute-start(f32[128,512]{1,0:T(8,128)} %copy.354), channel_id=1, source_target_pairs={{1,0},{2,1},{3,2},{4,3},{5,4},{6,5},{7,6},{8,7},{9,8},{10,9},{11,1... | collective-permute-start | bytes 786440 | tf_op jit(solution)/shard_map/ppermute | solution.py:22
  71.8 28.8 %collective-permute-start.9 = (f32[128,512]{1,0:T(8,128)}, f32[128,512]{1,0:T(8,128)}, u32[]{:S(2)}, u32[]{:S(2)}) collective-permute-start(f32[128,512]{1,0:T(8,128)} %copy.351), channel_id=1, source_target_pairs={{3,0},{4,1},{5,2},{6,3},{7,4},{8,5},{9,6},{10,7},{11,8},{12,9},{13... | collective-permute-start | bytes 786440 | tf_op jit(solution)/shard_map/ppermute | solution.py:22
  88.9 23.0 %all-to-all-start = ((bf16[16,2,4096]{2,1,0:T(2,128)(2,1)}), bf16[16,2,4096]{2,1,0:T(2,128)(2,1)S(1)}, u32[]{:S(2)}, u32[]{:S(2)}) async-start(bf16[16,2,4096]{2,1,0:T(2,128)(2,1)} %reshape.347), calls=%async_computation | async-start | bytes 524288 | tf_op jit(solution)/shard_map/all_to_all | solution.py:103
  101.9 18.4 %copy-start.21 = (bf16[128,512]{1,0:T(8,128)(2,1)}, bf16[128,512]{1,0:T(8,128)(2,1)S(1)}, u32[]{:S(2)}) copy-start(bf16[128,512]{1,0:T(8,128)(2,1)S(1)} %add_convert_fusion) | copy-start | bytes 393220
  118.0 24.1 %copy-start.33 = (s32[16]{0:T(128)S(1)}, s32[16]{0:T(128)}, u32[]{:S(2)}) copy-start(s32[16]{0:T(128)} %get-tuple-element.31) | copy-start | bytes 196
  121.1 15.9 %all-to-all-start.3 = ((f32[1,16,512]{2,0,1:T(1,128)}), f32[1,16,512]{2,0,1:T(1,128)S(1)}, u32[]{:S(2)}, u32[]{:S(2)}) async-start(f32[1,16,512]{2,0,1:T(1,128)} %copy.358), calls=%async_computation.3 | async-start | bytes 65536 | tf_op jit(solution)/shard_map/all_to_all | solution.py:179
  127.4 15.5 %collective-permute-start.5 = (bf16[128,512]{1,0:T(8,128)(2,1)S(1)}, bf16[128,512]{1,0:T(8,128)(2,1)S(1)}, u32[]{:S(2)}, u32[]{:S(2)}) collective-permute-start(bf16[128,512]{1,0:T(8,128)(2,1)S(1)} %fusion.29), channel_id=1, source_target_pairs={{0,1},{1,2},{2,3},{3,4},{4,5},{5,6},{6,7},{7,8},{8,9},{9,10},{10,1... | collective-permute-start | bytes 393224 | tf_op jit(solution)/shard_map/ppermute | solution.py:22
  130.9 12.0 %collective-permute-start.4 = (bf16[128,512]{1,0:T(8,128)(2,1)S(1)}, bf16[128,512]{1,0:T(8,128)(2,1)}, u32[]{:S(2)}, u32[]{:S(2)}) collective-permute-start(bf16[128,512]{1,0:T(8,128)(2,1)S(1)} %fusion.29), channel_id=1, source_target_pairs={{0,2},{1,3},{2,4},{3,5},{4,6},{5,7},{6,8},{7,9},{8,10},{9,11},{10,... | collective-permute-start | bytes 393224 | tf_op jit(solution)/shard_map/ppermute | solution.py:22
  134.7 8.2 %collective-permute-start.3 = (bf16[128,512]{1,0:T(8,128)(2,1)S(1)}, bf16[128,512]{1,0:T(8,128)(2,1)}, u32[]{:S(2)}, u32[]{:S(2)}) collective-permute-start(bf16[128,512]{1,0:T(8,128)(2,1)S(1)} %fusion.29), channel_id=1, source_target_pairs={{0,3},{1,4},{2,5},{3,6},{4,7},{5,8},{6,9},{7,10},{8,11},{9,12},{10... | collective-permute-start | bytes 393224 | tf_op jit(solution)/shard_map/ppermute | solution.py:22
  137.0 53.5 %all-to-all-start.2 = ((f32[1,16,8192]{2,0,1:T(1,128)}), f32[1,16,8192]{2,0,1:T(1,128)}, u32[]{:S(2)}, u32[]{:S(2)}) async-start(f32[1,16,8192]{2,0,1:T(1,128)} %reshape.345), calls=%async_computation.2 | async-start | bytes 1048576 | tf_op jit(solution)/shard_map/all_to_all | solution.py:172
  160.5 13.4 %copy-start.10 = (bf16[8,128,512]{1,2,0:T(8,128)(2,1)S(1)}, bf16[8,128,512]{1,2,0:T(8,128)(2,1)}, u32[]{:S(2)}) copy-start(bf16[8,128,512]{1,2,0:T(8,128)(2,1)} %copy-done.9) | copy-start | bytes 3145732
  168.8 10.8 %collective-permute-start.7 = (f32[128,512]{1,0:T(8,128)}, f32[128,512]{1,0:T(8,128)}, u32[]{:S(2)}, u32[]{:S(2)}) collective-permute-start(f32[128,512]{1,0:T(8,128)} %copy.341), channel_id=1, source_target_pairs={{2,0},{3,1},{4,2},{5,3},{6,4},{7,5},{8,6},{9,7},{10,8},{11,9},{12,... | collective-permute-start | bytes 786440 | tf_op jit(solution)/shard_map/ppermute | solution.py:22
  170.2 14.6 %collective-permute-start.8 = (f32[128,512]{1,0:T(8,128)}, f32[128,512]{1,0:T(8,128)}, u32[]{:S(2)}, u32[]{:S(2)}) collective-permute-start(f32[128,512]{1,0:T(8,128)} %copy.342), channel_id=1, source_target_pairs={{1,0},{2,1},{3,2},{4,3},{5,4},{6,5},{7,6},{8,7},{9,8},{10,9},{11,1... | collective-permute-start | bytes 786440 | tf_op jit(solution)/shard_map/ppermute | solution.py:22
  172.6 16.1 %collective-permute-start.6 = (f32[128,512]{1,0:T(8,128)}, f32[128,512]{1,0:T(8,128)}, u32[]{:S(2)}, u32[]{:S(2)}) collective-permute-start(f32[128,512]{1,0:T(8,128)} %copy.339), channel_id=1, source_target_pairs={{3,0},{4,1},{5,2},{6,3},{7,4},{8,5},{9,6},{10,7},{11,8},{12,9},{13... | collective-permute-start | bytes 786440 | tf_op jit(solution)/shard_map/ppermute | solution.py:22
  (36 other events, 127.7 us)
where the time goes:
time: 201 us; the launch traced here: 199 us
  local copies, waits for them, and re-layouts  78.7 us (39%)
  starting transfers between devices  55.3 us (28%)
  matrix products  35.8 us (18%)
  other arithmetic  18.7 us (9%)
  waiting for transfers between devices  9.09 us (5%)
    ppermute x12, starting transfers between devices, shifted(): return lax.ppermute(array, axis, pairs)  30.2 us
    unnamed x104, local copies, waits for them, and re-layouts  26.6 us
    sub x4, matrix products, window_grads(): weights = jnp.where(allowed[None], jnp.exp(scores - row_top), 0.0)  13.2 us
    all_to_all x1, starting transfers between devices, per_device(): lax.all_to_all(send_down, 'ctx', split_axis=1, concat_axis=1, tiled=True)  9.35 us
    ppermute x12, waiting for transfers between devices, shifted(): return lax.ppermute(array, axis, pairs)  9.08 us
    slice x4, local copies, waits for them, and re-layouts, per_device(): value_gradient[offset:offset + row_count]  6.39 us
    slice x4, local copies, waits for them, and re-layouts, per_device(): key_gradient[offset:offset + row_count]  6.3 us
    all_to_all x1, starting transfers between devices, per_device(): lax.all_to_all(up_gradient.reshape(slot_count, devices, -1), 'ctx', split...  6.02 us
  transfers between devices with their start and end apart: 16, of which 2 were waited for; matrix products, arithmetic and copies ran while one was open for 55% of the time, Pallas kernels for 0%

commit v1 on v0

v1 whole, which is shorter than its diff:
```python
import functools

import jax
import jax.numpy as jnp
from jax import lax
from jax.experimental import pallas as pl
from jax.experimental.pallas import tpu as pltpu
from jax.sharding import PartitionSpec as P

HEAD_SIZE = 128
R = 16
TILE = 128
SEGMAX = 512
ADAPTER_SCALE = 2.0
NEG_BIG = -1e30
LOG2E = 1.4426950408889634
NT = (((1,), (1,)), ((), ()))
F32 = jnp.float32
BF16 = jnp.bfloat16


def dot(a, b):
    return jnp.dot(a, b, preferred_element_type=F32)


def dot_nt(a, b):
    return lax.dot_general(a, b, NT, preferred_element_type=F32)


def kernel(
    n, reach, seg_tiles, seg_tenant, hidden_hbm, q_hbm, keys_hbm, frozen_hbm, do_hbm, down_hbm, up_ref,
    dq_hbm, dk_ref, dv_ref, gd_ref, gu_ref,
    hidden, q, do, frozen, down, kwin, vwin, upf, send_a, recv_a, pbuf, dsbuf, dqv, tri,
    dv_own, dv_send, dv_recv, dk_own, dk_send, dk_recv, send_g, recv_g, pick, ten,
    load_sem, dq_sem, k_s, k_r, v_s, v_r, a_s, a_r, dv_s, dv_r, dk_s, dk_r, g_s, g_r,
):
    me = lax.axis_index("ctx")
    adapters, _, piece = down.shape
    up_piece = upf.shape[1]
    up_lanes = min(up_piece, 128)
    up_rows = up_piece // up_lanes
    kvw = frozen.shape[1]
    groups = kvw // HEAD_SIZE
    gw = q.shape[1] // groups
    heads = gw // HEAD_SIZE
    per_row = kvw // up_lanes
    segs = seg_tiles.shape[0]
    window = (reach + 1) * TILE
    scale = HEAD_SIZE ** -0.5

    pairs = (
        (keys_hbm, kwin.at[0]), (down_hbm, down), (q_hbm, q), (do_hbm, do),
        (hidden_hbm, hidden), (frozen_hbm, frozen),
    )
    loads = [pltpu.make_async_copy(a, b, load_sem.at[i]) for i, (a, b) in enumerate(pairs)]
    for load in loads:
        load.start()

    barrier = pltpu.get_barrier_semaphore()

    def greet(i, carry):
        pl.semaphore_signal(
            barrier, inc=1, device_id={"ctx": lax.rem(me + i, n)}, device_id_type=pl.DeviceIdType.MESH
        )
        return carry

    lax.fori_loop(1, n, greet, 0)

    ends = []
    total = jnp.int32(0)
    for i in range(segs):
        total = total + seg_tiles[i]
        ends.append(total)

    def segment(j):
        s = jnp.int32(0)
        for end in ends:
            s = s + (end <= j).astype(jnp.int32)
        return s

    def note(j, carry):
        ten[j] = seg_tenant[jnp.minimum(segment(j), segs - 1)]
        return carry

    lax.fori_loop(0, n, note, 0)
    my_segment = segment(me)
    bias = [None]
    for d in range(1, reach + 1):
        same = jnp.logical_and(me >= d, segment(me - d) == my_segment)
        bias.append(jnp.where(same, jnp.float32(0), jnp.float32(NEG_BIG)))
    w_place = lax.broadcasted_iota(jnp.int32, (TILE, TILE), 0)
    t_place = lax.broadcasted_iota(jnp.int32, (TILE, TILE), 1)
    tri[...] = jnp.where(w_place <= t_place, 0.0, NEG_BIG).astype(F32)
    upf[...] = up_ref[...].astype(F32)

    for d in range(1, reach + 1):
        @pl.when(me < d)
        def _():
            kwin[d] = jnp.zeros((TILE, kvw), BF16)
            vwin[d] = jnp.zeros((TILE, kvw), BF16)

        @pl.when(me + d >= n)
        def _():
            for g in range(groups):
                dv_recv[g, d - 1] = jnp.zeros((TILE, HEAD_SIZE), BF16)
                dk_recv[g, d - 1] = jnp.zeros((TILE, HEAD_SIZE), BF16)

    def forward(win, d, ss, rs):
        return pltpu.make_async_remote_copy(
            src_ref=win.at[0], dst_ref=win.at[d], send_sem=ss.at[d - 1], recv_sem=rs.at[d - 1],
            device_id={"ctx": lax.rem(me + d, n)}, device_id_type=pl.DeviceIdType.MESH,
        )

    def backward(src, dst, g, d, ss, rs):
        at = g * reach + d - 1
        return pltpu.make_async_remote_copy(
            src_ref=src.at[g, d - 1], dst_ref=dst.at[g, d - 1], send_sem=ss.at[at], recv_sem=rs.at[at],
            device_id={"ctx": lax.rem(me + n - d, n)}, device_id_type=pl.DeviceIdType.MESH,
        )

    def rows(j):
        return pl.ds(pl.multiple_of(j * R, R), R)

    def scatter(src, dst, peer, ss, rs):
        return pltpu.make_async_remote_copy(
            src_ref=src.at[rows(peer)], dst_ref=dst.at[rows(me)], send_sem=ss.at[peer], recv_sem=rs.at[me],
            device_id={"ctx": peer}, device_id_type=pl.DeviceIdType.MESH,
        )

    def arrived(dst, source, ss, rs):
        return pltpu.make_async_remote_copy(
            src_ref=dst.at[rows(source)], dst_ref=dst.at[rows(source)], send_sem=ss.at[source],
            recv_sem=rs.at[source], device_id={"ctx": source}, device_id_type=pl.DeviceIdType.MESH,
        )

    def wait_arrivals(dst, ss, rs):
        def one(i, carry):
            arrived(dst, lax.rem(me + i, n), ss, rs).wait_recv()
            return carry

        lax.fori_loop(1, n, one, 0)

    def wait_sends(src, dst, ss, rs):
        def one(i, carry):
            scatter(src, dst, lax.rem(me + i, n), ss, rs).wait_send()
            return carry

        lax.fori_loop(1, n, one, 0)

    row_id = lax.broadcasted_iota(jnp.int32, (R, up_lanes), 0)

    def factors(j):
        tenant = ten[j]
        row = upf[pl.ds(tenant, 1), :]
        tail = jnp.zeros((R, up_lanes), F32)
        for k in range(up_rows):
            tail = jnp.where(row_id == k, row[:, k * up_lanes:(k + 1) * up_lanes], tail)
        return down[tenant], tail.astype(BF16)

    loads[0].wait()
    loads[1].wait()
    pl.semaphore_wait(barrier, n - 1)
    for d in range(1, reach + 1):
        @pl.when(me + d < n)
        def _():
            forward(kwin, d, k_s, k_r).start()

    def give(i, carry):
        peer = lax.rem(me + i, n)
        mat, tail = factors(peer)
        send_a[rows(peer), 0:piece] = mat
        send_a[rows(peer), piece:piece + up_lanes] = tail
        scatter(send_a, recv_a, peer, a_s, a_r).start()
        return carry

    lax.fori_loop(1, n, give, 0)
    mat, tail = factors(me)
    recv_a[rows(me), 0:piece] = mat
    recv_a[rows(me), piece:piece + up_lanes] = tail

    col = lax.broadcasted_iota(jnp.int32, (1, n * R), 1)
    col_tile = jnp.right_shift(col, 4)
    col_rank = jnp.bitwise_and(col, R - 1)
    col_tenant = jnp.zeros((1, n * R), jnp.int32)
    for j in range(n):
        col_tenant = jnp.where(col_tile == j, ten[j], col_tenant)
    blocks = adapters // 16
    for b in range(blocks):
        line = lax.broadcasted_iota(jnp.int32, (16 * R, n * R), 0)
        hit = jnp.logical_and(
            col_tenant == b * 16 + jnp.right_shift(line, 4), col_rank == jnp.bitwise_and(line, R - 1)
        )
        pick[b * 16 * R:(b + 1) * 16 * R, :] = jnp.where(hit, 1.0, 0.0).astype(BF16)

    loads[2].wait()
    loads[3].wait()
    for d in range(1, reach + 1):
        @pl.when(me >= d)
        def _():
            forward(kwin, d, k_s, k_r).wait_recv()

    def lanes(g, width):
        return pl.ds(pl.multiple_of(g * width, width), width)

    def stack(ref, g):
        part = ref[:, lanes(g, gw)]
        return jnp.concatenate([part[:, h * HEAD_SIZE:(h + 1) * HEAD_SIZE] for h in range(heads)], axis=0)

    def first(g, carry):
        kg = kwin[:, :, lanes(g, HEAD_SIZE)].reshape(window, HEAD_SIZE)
        qg = q[:, lanes(g, gw)]
        for h in range(heads):
            s = dot_nt(kg, qg[:, h * HEAD_SIZE:(h + 1) * HEAD_SIZE])
            parts = [s[0:TILE] + tri[...]]
            for d in range(1, reach + 1):
                parts.append(s[d * TILE:(d + 1) * TILE] + bias[d])
            s = jnp.concatenate(parts, axis=0)
            top = jnp.max(s, axis=0, keepdims=True)
            e = jnp.exp2((s - top) * (scale * LOG2E))
            inv = 1.0 / jnp.sum(e, axis=0, keepdims=True)
            pbuf[g, :, h * HEAD_SIZE:(h + 1) * HEAD_SIZE] = (e * inv).astype(BF16)
        dv = dot(pbuf[g], stack(do, g))
        dv_own[:, lanes(g, HEAD_SIZE)] = dv[0:TILE]
        for d in range(1, reach + 1):
            dv_send[g, d - 1] = dv[d * TILE:(d + 1) * TILE].astype(BF16)

            @pl.when(me >= d)
            def _():
                backward(dv_send, dv_recv, g, d, dv_s, dv_r).start()
        return carry

    lax.fori_loop(0, groups, first, 0)

    loads[4].wait()
    loads[5].wait()
    wait_arrivals(recv_a, a_s, a_r)
    per = max(1, 512 // piece)
    low_t = jnp.zeros((R, TILE), F32)
    for c in range(0, n, per):
        mats = [recv_a[j * R:(j + 1) * R, 0:piece] for j in range(c, c + per)]
        mats = mats[0] if per == 1 else jnp.concatenate(mats, axis=1)
        low_t = low_t + dot_nt(mats, hidden[:, c * piece:(c + per) * piece])
    low_half = low_t.astype(BF16)
    rank = lax.broadcasted_iota(jnp.int32, (R, n * R), 0)
    ups = []
    for k in range(per_row):
        hit = jnp.logical_and(col_rank < up_rows, col_tile * up_rows + col_rank == rank * per_row + k)
        ups.append(dot(jnp.where(hit, 1.0, 0.0).astype(BF16), recv_a[:, piece:piece + up_lanes]))
    up = jnp.concatenate(ups, axis=1)
    up_half = up.astype(BF16)
    low = jnp.concatenate([low_t, jnp.zeros((TILE - R, TILE), F32)], axis=0).T.astype(BF16)
    up_tall = jnp.concatenate([up, jnp.zeros((TILE - R, kvw), F32)], axis=0).astype(BF16)
    vwin[0] = (frozen[...].astype(F32) + ADAPTER_SCALE * dot(low, up_tall)).astype(BF16)
    for d in range(1, reach + 1):
        @pl.when(me + d < n)
        def _():
            forward(vwin, d, v_s, v_r).start()

    def gather_back(own, send, recv, out, ss, rs):
        for d in range(1, reach + 1):
            @pl.when(me + d < n)
            def _():
                for g in range(groups):
                    backward(send, recv, g, d, ss, rs).wait_recv()
        for g in range(groups):
            acc = own[:, g * HEAD_SIZE:(g + 1) * HEAD_SIZE]
            for d in range(1, reach + 1):
                acc = acc + recv[g, d - 1].astype(F32)
            out[:, g * HEAD_SIZE:(g + 1) * HEAD_SIZE] = acc.astype(BF16)

    gather_back(dv_own, dv_send, dv_recv, dv_ref, dv_s, dv_r)
    dv = dv_ref[...]
    grad_t = (ADAPTER_SCALE * dot_nt(up_half, dv)).astype(BF16)
    up_grad = ADAPTER_SCALE * dot(low_half, dv)
    for j in range(n):
        send_g[j * R:(j + 1) * R, 0:piece] = dot(grad_t, hidden[:, j * piece:(j + 1) * piece]).astype(BF16)
        tail = jnp.zeros((R, up_lanes), F32)
        for k in range(up_rows):
            r, c = divmod(j * up_rows + k, per_row)
            tail = jnp.where(row_id == k, up_grad[r:r + 1, c * up_lanes:(c + 1) * up_lanes], tail)
        send_g[j * R:(j + 1) * R, piece:piece + up_lanes] = tail.astype(BF16)

        @pl.when(me != j)
        def _():
            scatter(send_g, recv_g, j, g_s, g_r).start()

    recv_g[rows(me), :] = send_g[rows(me), :]

    for d in range(1, reach + 1):
        @pl.when(me >= d)
        def _():
            forward(vwin, d, v_s, v_r).wait_recv()

    def dq_out(g):
        return pltpu.make_async_copy(dqv.at[g], dq_hbm.at[:, lanes(g, gw)], dq_sem.at[g])

    def second(g, carry):
        kg = kwin[:, :, lanes(g, HEAD_SIZE)].reshape(window, HEAD_SIZE)
        vg = vwin[:, :, lanes(g, HEAD_SIZE)].reshape(window, HEAD_SIZE)
        dog = do[:, lanes(g, gw)]
        for h in range(heads):
            at = slice(h * HEAD_SIZE, (h + 1) * HEAD_SIZE)
            dp = dot_nt(vg, dog[:, at])
            p = pbuf[g, :, at].astype(F32)
            delta = jnp.sum(p * dp, axis=0, keepdims=True)
            dsbuf[:, at] = (p * ((dp - delta) * scale)).astype(BF16)
        ds = dsbuf[...]
        dk = dot(ds, stack(q, g))
        dk_own[:, lanes(g, HEAD_SIZE)] = dk[0:TILE]
        for d in range(1, reach + 1):
            dk_send[g, d - 1] = dk[d * TILE:(d + 1) * TILE].astype(BF16)

            @pl.when(me >= d)
            def _():
                backward(dk_send, dk_recv, g, d, dk_s, dk_r).start()
        dq_t = dot(kg.astype(F32).T.astype(BF16), dsbuf[...])
        for h in range(heads):
            at = slice(h * HEAD_SIZE, (h + 1) * HEAD_SIZE)
            dqv[g, :, at] = dq_t[:, at].T.astype(BF16)
        dq_out(g).start()
        return carry

    lax.fori_loop(0, groups, second, 0)

    wait_arrivals(recv_g, g_s, g_r)
    line = lax.broadcasted_iota(jnp.int32, (16, n * R), 0)
    for b in range(blocks):
        out = dot(pick[b * 16 * R:(b + 1) * 16 * R, :], recv_g[:, 0:piece])
        gd_ref[b * 16:(b + 1) * 16] = out.reshape(16, R, piece)
        for k in range(up_rows):
            hit = jnp.logical_and(col_tenant == b * 16 + line, col_rank == k)
            gu_ref[b * 16:(b + 1) * 16, k * up_lanes:(k + 1) * up_lanes] = dot(
                jnp.where(hit, 1.0, 0.0).astype(BF16), recv_g[:, piece:piece + up_lanes]
            )
    gather_back(dk_own, dk_send, dk_recv, dk_ref, dk_s, dk_r)

    for g in range(groups):
        dq_out(g).wait()
    for d in range(1, reach + 1):
        @pl.when(me + d < n)
        def _():
            forward(kwin, d, k_s, k_r).wait_send()
            forward(vwin, d, v_s, v_r).wait_send()

        @pl.when(me >= d)
        def _():
            for g in range(groups):
                backward(dv_send, dv_recv, g, d, dv_s, dv_r).wait_send()
                backward(dk_send, dk_recv, g, d, dk_s, dk_r).wait_send()

    wait_sends(send_a, recv_a, a_s, a_r)
    wait_sends(send_g, recv_g, g_s, g_r)


def per_device(
    hidden_in, queries, keys, frozen_values, d_out, adapter_down, adapter_up, seg_tiles, seg_tenant
):
    n = lax.axis_size("ctx")
    row_count, d_model = hidden_in.shape
    reach = (SEGMAX - TILE) // row_count
    adapters, piece, _ = adapter_down.shape
    up_piece = adapter_up.shape[1]
    kvw = keys.shape[1]
    qw = queries.shape[1]
    groups = kvw // HEAD_SIZE
    gw = qw // groups
    window = (reach + 1) * row_count
    wide = piece + min(up_piece, 128)
    vmem = pl.BlockSpec(memory_space=pltpu.VMEM)
    smem = pl.BlockSpec(memory_space=pltpu.SMEM)
    hbm = pl.BlockSpec(memory_space=pl.ANY)
    sem = pltpu.SemaphoreType.DMA
    terms = pltpu.VMEM((groups, reach, row_count, HEAD_SIZE), BF16)
    own = pltpu.VMEM((row_count, kvw), F32)
    a2a = pltpu.VMEM((n * R, wide), BF16)
    d_queries, d_keys, d_values, grad_down, grad_up = pl.pallas_call(
        functools.partial(kernel, n, reach),
        out_shape=(
            jax.ShapeDtypeStruct((row_count, qw), BF16),
            jax.ShapeDtypeStruct((row_count, kvw), BF16),
            jax.ShapeDtypeStruct((row_count, kvw), BF16),
            jax.ShapeDtypeStruct((adapters, R, piece), F32),
            jax.ShapeDtypeStruct((adapters, up_piece), F32),
        ),
        in_specs=[smem, smem, hbm, hbm, hbm, hbm, hbm, hbm, vmem],
        out_specs=(hbm, vmem, vmem, vmem, vmem),
        scratch_shapes=[
            pltpu.VMEM((row_count, d_model), BF16),
            pltpu.VMEM((row_count, qw), BF16),
            pltpu.VMEM((row_count, qw), BF16),
            pltpu.VMEM((row_count, kvw), BF16),
            pltpu.VMEM((adapters, R, piece), BF16),
            pltpu.VMEM((reach + 1, row_count, kvw), BF16),
            pltpu.VMEM((reach + 1, row_count, kvw), BF16),
            pltpu.VMEM((adapters, up_piece), F32),
            a2a,
            a2a,
            pltpu.VMEM((groups, window, gw), BF16),
            pltpu.VMEM((window, gw), BF16),
            pltpu.VMEM((groups, row_count, gw), BF16),
            pltpu.VMEM((TILE, TILE), F32),
            own, terms, terms,
            own, terms, terms,
            a2a,
            a2a,
            pltpu.VMEM((adapters * R, n * R), BF16),
            pltpu.SMEM((n,), jnp.int32),
            sem((6,)),
            sem((groups,)),
            sem((reach,)), sem((reach,)), sem((reach,)), sem((reach,)),
            sem((n,)), sem((n,)),
            sem((groups * reach,)), sem((groups * reach,)),
            sem((groups * reach,)), sem((groups * reach,)),
            sem((n,)), sem((n,)),
        ],
        compiler_params=pltpu.CompilerParams(
            collective_id=0, has_side_effects=True, vmem_limit_bytes=48 * 1024 * 1024
        ),
    )(
        seg_tiles, seg_tenant, hidden_in, queries, keys, frozen_values, d_out,
        jnp.swapaxes(adapter_down, 1, 2), adapter_up,
    )
    return (d_queries, d_keys, d_values, jnp.swapaxes(grad_down, 1, 2), grad_up)


def solution(mesh):
    placed = (
        P(("groups", "ctx"), None),
        P(("groups", "ctx"), None),
        P(("groups", "ctx"), None),
        P(("groups", "ctx"), None),
        P(("groups", "ctx"), None),
        P(None, "ctx", None),
        P(None, "ctx"),
        P("groups"),
        P("groups"),
    )
    return jax.shard_map(
        per_device,
        mesh=mesh,
        in_specs=placed,
        out_specs=(
            P(("groups", "ctx"), None),
            P(("groups", "ctx"), None),
            P(("groups", "ctx"), None),
            P("groups", "ctx", None),
            P("groups", "ctx"),
        ),
        check_vma=False,
    )
```

time: 201 us -> 62.7 us (0.31)
  local copies, waits for them, and re-layouts: 78.7 us -> 10.9 us
  starting transfers between devices: 55.3 us -> 0 us
  Pallas kernels: 0 us -> 50.8 us
  matrix products: 35.8 us -> 0 us
  other arithmetic: 18.7 us -> 0 us
  waiting for transfers between devices: 9.09 us -> 0 us
    pallas_call x0 -> x1, Pallas kernels: none -> 50.8 us  [per_device(): pl.pallas_call(functools.partial(kernel, n, reach), out_shape=(jax.ShapeD...]
    ppermute x12 -> x0, starting transfers between devices: 30.2 us -> none  [shifted(): return lax.ppermute(array, axis, pairs)]
    all_to_all x4 -> x0, starting transfers between devices: 25.1 us -> none  [the longest x1 9.35 us: per_device(): lax.all_to_all(send_down, 'ctx', split_axis=1, concat_axis=1, tiled=True)]
    dot_general x26 -> x0, matrix products: 22.6 us -> none  [the longest x4 5.96 us: window_grads(): jnp.einsum('gtw,wd->tgd', d_score, key_part, preferred_element_type=jnp.f...]
    slice x13 -> x0, local copies, waits for them, and re-layouts: 20.1 us -> none  [the longest x4 6.39 us: per_device(): value_gradient[offset:offset + row_count]]
    unnamed x104 -> x21, local copies, waits for them, and re-layouts: 26.6 us -> 10.9 us
    sub x4 -> x0, matrix products: 13.2 us -> none  [window_grads(): weights = jnp.where(allowed[None], jnp.exp(scores - row_top), 0.0)]
    reshape x3 -> x0, local copies, waits for them, and re-layouts: 10.9 us -> none  [the longest x1 4.69 us: per_device(): down_rows = adapter_down.reshape(adapter_count, -1)]
  transfers between devices with their start and end apart: 16 -> 0, of which waited for: 2 -> 0; matrix products, arithmetic and copies ran while one was open for 55% -> 0% of each run, Pallas kernels for 0% -> 0%
where the time goes in v1:
time: 62.7 us; the launch traced here: 62.3 us
  Pallas kernels  50.8 us (81%)
  local copies, waits for them, and re-layouts  10.9 us (17%)
  between operations  0.66 us (1%)
    pallas_call x1, Pallas kernels, per_device(): pl.pallas_call(functools.partial(kernel, n, reach), out_shape=(jax.ShapeD...  50.8 us
    unnamed x21, local copies, waits for them, and re-layouts  10.9 us

profile of v1, /device:TPU:1, one launch (start us, length us, event | category | flops | bytes accessed | tf_op | source)
XLA Modules:
  0.0 62.3 jit_solution(4403654982825085491)
XLA Ops:
  0.6 0.0 copy-start
  0.6 1.2 %copy-done = bf16[128,4096]{1,0:T(8,128)(2,1)S(1)} copy-done((bf16[128,4096]{1,0:T(8,128)(2,1)S(1)}, bf16[128,4096]{1,0:T(8,128)(2,1)}, u32[]{:S(2)}) %copy-start) | copy-done | bytes 1048600
  1.9 0.0 copy-start.1
  1.9 1.2 %copy-done.1 = bf16[128,4096]{1,0:T(8,128)(2,1)S(1)} copy-done((bf16[128,4096]{1,0:T(8,128)(2,1)S(1)}, bf16[128,4096]{1,0:T(8,128)(2,1)}, u32[]{:S(2)}) %copy-start.1) | copy-done | bytes 1048600
  3.1 0.0 copy-start.2
  3.1 0.9 %copy-done.2 = bf16[16,512,16]{1,2,0:T(8,128)(2,1)S(1)} copy-done((bf16[16,512,16]{1,2,0:T(8,128)(2,1)S(1)}, bf16[16,512,16]{1,2,0:T(8,128)(2,1)}, u32[]{:S(2)}) %copy-start.2) | copy-done | bytes 262168
  4.0 0.0 copy-start.3
  4.0 0.9 %copy-done.3 = bf16[128,512]{1,0:T(8,128)(2,1)S(1)} copy-done((bf16[128,512]{1,0:T(8,128)(2,1)S(1)}, bf16[128,512]{1,0:T(8,128)(2,1)}, u32[]{:S(2)}) %copy-start.3) | copy-done | bytes 131096
  4.9 0.0 copy-start.4
  4.9 0.9 %copy-done.4 = bf16[128,512]{1,0:T(8,128)(2,1)S(1)} copy-done((bf16[128,512]{1,0:T(8,128)(2,1)S(1)}, bf16[128,512]{1,0:T(8,128)(2,1)}, u32[]{:S(2)}) %copy-start.4) | copy-done | bytes 131096
  5.8 0.0 copy-start.5
  5.8 0.7 %copy-done.5 = bf16[16,512]{1,0:T(8,128)(2,1)S(1)} copy-done((bf16[16,512]{1,0:T(8,128)(2,1)S(1)}, bf16[16,512]{1,0:T(8,128)(2,1)}, u32[]{:S(2)}) %copy-start.5) | copy-done | bytes 16408
  6.6 0.0 copy-start.6
  6.6 0.7 %copy-done.6 = s32[8]{0:T(128)S(1)} copy-done((s32[8]{0:T(128)S(1)}, s32[8]{0:T(128)}, u32[]{:S(2)}) %copy-start.6) | copy-done | bytes 56
  7.2 0.0 copy-start.7
  7.2 0.7 %copy-done.7 = s32[8]{0:T(128)S(1)} copy-done((s32[8]{0:T(128)S(1)}, s32[8]{0:T(128)}, u32[]{:S(2)}) %copy-start.7) | copy-done | bytes 56
  7.9 50.8 %shard_map.128 = (bf16[128,4096]{1,0:T(8,128)(2,1)S(1)}, bf16[128,512]{1,0:T(8,128)(2,1)S(1)}, bf16[128,512]{1,0:T(8,128)(2,1)S(1)}, f32[16,16,512]{2,1,0:T(8,128)S(1)}, f32[16,512]{1,0:T(8,128)S(1)}) custom-call(s32[8]{0:T(128)S(1)} %copy-done.6, s32[8]{0:T(128)S(1)} %copy-done.7, bf16[128,8192]{1,0:T(8,128)(2,1)} %hidden_hbm.1, ...), custom_call_target="tpu_custom_call" | custom-call | tf_op jit(solution)/shard_map/pallas_call | solution.py:376
  58.6 1.0 %copy.19 = bf16[128,4096]{1,0:T(8,128)(2,1)} copy(bf16[128,4096]{1,0:T(8,128)(2,1)S(1)} %get-tuple-element.20) | data formatting | bytes 2097152
  59.6 0.7 %copy.20 = bf16[128,512]{1,0:T(8,128)(2,1)} copy(bf16[128,512]{1,0:T(8,128)(2,1)S(1)} %get-tuple-element.21) | data formatting | bytes 262144
  60.3 0.7 %copy.21 = bf16[128,512]{1,0:T(8,128)(2,1)} copy(bf16[128,512]{1,0:T(8,128)(2,1)S(1)} %get-tuple-element.22) | data formatting | bytes 262144
  60.9 0.8 %copy.22 = f32[16,512,16]{1,2,0:T(8,128)} copy(f32[16,512,16]{1,2,0:T(8,128)S(1)} %bitcast.2) | data formatting | bytes 1048576
  61.7 0.6 copy.23
Async XLA Ops:
  0.6 1.2 %copy-start = (bf16[128,4096]{1,0:T(8,128)(2,1)S(1)}, bf16[128,4096]{1,0:T(8,128)(2,1)}, u32[]{:S(2)}) copy-start(bf16[128,4096]{1,0:T(8,128)(2,1)} %q_hbm.1) | copy-start | bytes 3145732
  1.9 1.2 %copy-start.1 = (bf16[128,4096]{1,0:T(8,128)(2,1)S(1)}, bf16[128,4096]{1,0:T(8,128)(2,1)}, u32[]{:S(2)}) copy-start(bf16[128,4096]{1,0:T(8,128)(2,1)} %do_hbm.1) | copy-start | bytes 3145732
  3.1 0.9 %copy-start.2 = (bf16[16,512,16]{1,2,0:T(8,128)(2,1)S(1)}, bf16[16,512,16]{1,2,0:T(8,128)(2,1)}, u32[]{:S(2)}) copy-start(bf16[16,512,16]{1,2,0:T(8,128)(2,1)} %param.14) | copy-start | bytes 786436
  4.0 0.9 %copy-start.3 = (bf16[128,512]{1,0:T(8,128)(2,1)S(1)}, bf16[128,512]{1,0:T(8,128)(2,1)}, u32[]{:S(2)}) copy-start(bf16[128,512]{1,0:T(8,128)(2,1)} %keys_hbm.1) | copy-start | bytes 393220
  4.9 0.9 %copy-start.4 = (bf16[128,512]{1,0:T(8,128)(2,1)S(1)}, bf16[128,512]{1,0:T(8,128)(2,1)}, u32[]{:S(2)}) copy-start(bf16[128,512]{1,0:T(8,128)(2,1)} %frozen_hbm.1) | copy-start | bytes 393220
  5.8 0.7 %copy-start.5 = (bf16[16,512]{1,0:T(8,128)(2,1)S(1)}, bf16[16,512]{1,0:T(8,128)(2,1)}, u32[]{:S(2)}) copy-start(bf16[16,512]{1,0:T(8,128)(2,1)} %up_ref.1) | copy-start | bytes 49156
  6.6 0.7 %copy-start.6 = (s32[8]{0:T(128)S(1)}, s32[8]{0:T(128)}, u32[]{:S(2)}) copy-start(s32[8]{0:T(128)} %seg_tiles.1) | copy-start | bytes 100
  7.2 0.7 %copy-start.7 = (s32[8]{0:T(128)S(1)}, s32[8]{0:T(128)}, u32[]{:S(2)}) copy-start(s32[8]{0:T(128)} %seg_tenant.1) | copy-start | bytes 100

commit v2 on v1

--- a/solution.py
+++ b/solution.py
@@ -28,18 +28,20 @@
 
 
 def kernel(
-    n, reach, seg_tiles, seg_tenant, hidden_hbm, q_hbm, keys_hbm, frozen_hbm, do_hbm, down_hbm, up_ref,
+    n, reach, tiles_hbm, tenant_hbm, hidden_hbm, q_hbm, keys_hbm, frozen_hbm, do_hbm, down_hbm, up_hbm,
     dq_hbm, dk_ref, dv_ref, gd_ref, gu_ref,
-    hidden, q, do, frozen, down, kwin, vwin, upf, send_a, recv_a, pbuf, dsbuf, dqv, tri,
-    dv_own, dv_send, dv_recv, dk_own, dk_send, dk_recv, send_g, recv_g, pick, ten,
-    load_sem, dq_sem, k_s, k_r, v_s, v_r, a_s, a_r, dv_s, dv_r, dk_s, dk_r, g_s, g_r,
+    seg_tiles, seg_tenant, up_in, hidden, q, do, down, kwin, fwin, lwin, vwin, upf, send_a, recv_a, pbuf, dsbuf, dqv, tri,
+    dv_buf, dk_buf, send_g, recv_g, pick, ten,
+    load_sem, dq_sem, k_s, k_r, f_s, f_r, l_s, l_r, a_s, a_r, dv_s, dv_r, dk_s, dk_r, g_s, g_r,
 ):
     me = lax.axis_index("ctx")
+    odd = lax.rem(me, 2)
+    partner = me + 1 - 2 * odd
     adapters, _, piece = down.shape
     up_piece = upf.shape[1]
     up_lanes = min(up_piece, 128)
     up_rows = up_piece // up_lanes
-    kvw = frozen.shape[1]
+    kvw = kwin.shape[2]
     groups = kvw // HEAD_SIZE
     gw = q.shape[1] // groups
     heads = gw // HEAD_SIZE
@@ -50,11 +52,12 @@
 
     pairs = (
         (keys_hbm, kwin.at[0]), (down_hbm, down), (q_hbm, q), (do_hbm, do),
-        (hidden_hbm, hidden), (frozen_hbm, frozen),
+        (hidden_hbm, hidden), (frozen_hbm, fwin.at[0]),
+        (tiles_hbm, seg_tiles), (tenant_hbm, seg_tenant), (up_hbm, up_in),
     )
     loads = [pltpu.make_async_copy(a, b, load_sem.at[i]) for i, (a, b) in enumerate(pairs)]
-    for load in loads:
-        load.start()
+    for i in (6, 7, 0, 8, 1, 2, 3, 4, 5):
+        loads[i].start()
 
     barrier = pltpu.get_barrier_semaphore()
 
@@ -66,6 +69,8 @@
 
     lax.fori_loop(1, n, greet, 0)
 
+    loads[6].wait()
+    loads[7].wait()
     ends = []
     total = jnp.int32(0)
     for i in range(segs):
@@ -91,32 +96,155 @@
     w_place = lax.broadcasted_iota(jnp.int32, (TILE, TILE), 0)
     t_place = lax.broadcasted_iota(jnp.int32, (TILE, TILE), 1)
     tri[...] = jnp.where(w_place <= t_place, 0.0, NEG_BIG).astype(F32)
-    upf[...] = up_ref[...].astype(F32)
+    loads[8].wait()
+    upf[...] = up_in[...].astype(F32)
 
     for d in range(1, reach + 1):
         @pl.when(me < d)
         def _():
             kwin[d] = jnp.zeros((TILE, kvw), BF16)
-            vwin[d] = jnp.zeros((TILE, kvw), BF16)
-
-        @pl.when(me + d >= n)
-        def _():
-            for g in range(groups):
-                dv_recv[g, d - 1] = jnp.zeros((TILE, HEAD_SIZE), BF16)
-                dk_recv[g, d - 1] = jnp.zeros((TILE, HEAD_SIZE), BF16)
-
-    def forward(win, d, ss, rs):
+            fwin[d] = jnp.zeros((TILE, kvw), BF16)
+            lwin[d] = jnp.zeros((R, TILE), BF16)
+
+    def clear(ref):
+        ref[...] = jnp.zeros(ref.shape, ref.dtype)
+
+    @pl.when(me + 2 >= n)
+    def _():
+        clear(dv_buf[6])
+        clear(dk_buf[6])
+
+    straight = jnp.logical_or(odd == 0, me + 3 < n)
+
+    @pl.when(jnp.logical_not(straight))
+    def _():
+        clear(dv_buf[7])
+        clear(dk_buf[7])
+
+    def remote(src, dst, ss, rs, peer):
         return pltpu.make_async_remote_copy(
-            src_ref=win.at[0], dst_ref=win.at[d], send_sem=ss.at[d - 1], recv_sem=rs.at[d - 1],
-            device_id={"ctx": lax.rem(me + d, n)}, device_id_type=pl.DeviceIdType.MESH,
+            src_ref=src, dst_ref=dst, send_sem=ss, recv_sem=rs,
+            device_id={"ctx": peer}, device_id_type=pl.DeviceIdType.MESH,
         )
 
-    def backward(src, dst, g, d, ss, rs):
-        at = g * reach + d - 1
-        return pltpu.make_async_remote_copy(
-            src_ref=src.at[g, d - 1], dst_ref=dst.at[g, d - 1], send_sem=ss.at[at], recv_sem=rs.at[at],
-            device_id={"ctx": lax.rem(me + n - d, n)}, device_id_type=pl.DeviceIdType.MESH,
-        )
+    def near(win, ss, rs):
+        return remote(win.at[0], win.at[1], ss.at[0], rs.at[0], partner)
+
+    def across(win, ss, rs):
+        return remote(win.at[0], win.at[2], ss.at[1], rs.at[1], lax.rem(me + 2, n))
+
+    def far(win, ss, rs):
+        return remote(win.at[0], win.at[3], ss.at[2], rs.at[2], lax.rem(me + 3, n))
+
+    def pass_on(win, ss, rs):
+        at = 3 - 2 * odd
+        return remote(win.at[2], win.at[at], ss.at[3], rs.at[at - 1], partner)
+
+    far_too = jnp.logical_and(odd == 1, me + 3 < n)
+
+    def spread(win, ss, rs):
+        @pl.when(me + 2 < n)
+        def _():
+            across(win, ss, rs).start()
+
+        @pl.when(far_too)
+        def _():
+            far(win, ss, rs).start()
+
+        @pl.when(odd == 0)
+        def _():
+            near(win, ss, rs).start()
+
+    def relay(win, ss, rs):
+        @pl.when(me >= 2)
+        def _():
+            across(win, ss, rs).wait_recv()
+            pass_on(win, ss, rs).start()
+
+    def settle(win, ss, rs):
+        @pl.when(me >= 1)
+        def _():
+            near(win, ss, rs).wait_recv()
+
+        @pl.when(me >= 3)
+        def _():
+            far(win, ss, rs).wait_recv()
+
+    def spread_sent(win, ss, rs):
+        @pl.when(me + 2 < n)
+        def _():
+            across(win, ss, rs).wait_send()
+
+        @pl.when(far_too)
+        def _():
+            far(win, ss, rs).wait_send()
+
+        @pl.when(odd == 0)
+        def _():
+            near(win, ss, rs).wait_send()
+
+        @pl.when(me >= 2)
+        def _():
+            pass_on(win, ss, rs).wait_send()
+
+    def meet(buf, ss, rs, g):
+        return remote(buf[2].at[g], buf[5].at[g], ss.at[0, g], rs.at[0, g], partner)
+
+    def back(buf, ss, rs, g):
+        return remote(buf[4].at[g], buf[6].at[g], ss.at[1, g], rs.at[1, g], lax.rem(me + n - 2, n))
+
+    def direct(buf, ss, rs, g):
+        return remote(buf[3].at[g], buf[7].at[g], ss.at[2, g], rs.at[2, g], lax.rem(me + n - 3 + 2 * odd, n))
+
+    has_direct = jnp.logical_or(odd == 1, me >= 3)
+
+    def send_terms(buf, ss, rs, g, terms):
+        own, mid = buf[0], buf[1]
+        one, two, three = (terms[d * TILE:(d + 1) * TILE] for d in (1, 2, 3))
+        own[g] = terms[0:TILE]
+        mid[g] = two
+        buf[2][g] = jnp.where(odd == 1, three, one).astype(BF16)
+        buf[3][g] = jnp.where(odd == 1, one, three).astype(BF16)
+
+        @pl.when(me >= 2)
+        def _():
+            meet(buf, ss, rs, g).start()
+
+        @pl.when(has_direct)
+        def _():
+            direct(buf, ss, rs, g).start()
+
+    def finish_terms(buf, ss, rs, g):
+        meet(buf, ss, rs, g).wait_recv()
+        buf[4][g] = (buf[1][g] + buf[5][g].astype(F32)).astype(BF16)
+        back(buf, ss, rs, g).start()
+
+    def gather_back(buf, out, ss, rs):
+        for g in range(groups):
+            @pl.when(straight)
+            def _():
+                direct(buf, ss, rs, g).wait_recv()
+
+            @pl.when(me + 2 < n)
+            def _():
+                back(buf, ss, rs, g).wait_recv()
+
+            acc = buf[0][g] + buf[6][g].astype(F32) + buf[7][g].astype(F32)
+            out[:, g * HEAD_SIZE:(g + 1) * HEAD_SIZE] = acc.astype(BF16)
+
+    def terms_sent(buf, ss, rs):
+        for g in range(groups):
+            @pl.when(me >= 2)
+            def _():
+                meet(buf, ss, rs, g).wait_send()
+                back(buf, ss, rs, g).wait_send()
+
+            @pl.when(has_direct)
+            def _():
+                direct(buf, ss, rs, g).wait_send()
+
+    def low_copy(d):
+        return remote(lwin.at[0], lwin.at[d], l_s.at[d - 1], l_r.at[d - 1], lax.rem(me + d, n))
 
     def rows(j):
         return pl.ds(pl.multiple_of(j * R, R), R)
@@ -160,10 +288,7 @@
     loads[0].wait()
     loads[1].wait()
     pl.semaphore_wait(barrier, n - 1)
-    for d in range(1, reach + 1):
-        @pl.when(me + d < n)
-        def _():
-            forward(kwin, d, k_s, k_r).start()
+    spread(kwin, k_s, k_r)
 
     def give(i, carry):
         peer = lax.rem(me + i, n)
@@ -177,6 +302,9 @@
     mat, tail = factors(me)
     recv_a[rows(me), 0:piece] = mat
     recv_a[rows(me), piece:piece + up_lanes] = tail
+    loads[5].wait()
+    spread(fwin, f_s, f_r)
+    relay(kwin, k_s, k_r)
 
     col = lax.broadcasted_iota(jnp.int32, (1, n * R), 1)
     col_tile = jnp.right_shift(col, 4)
@@ -194,10 +322,7 @@
 
     loads[2].wait()
     loads[3].wait()
-    for d in range(1, reach + 1):
-        @pl.when(me >= d)
-        def _():
-            forward(kwin, d, k_s, k_r).wait_recv()
+    settle(kwin, k_s, k_r)
 
     def lanes(g, width):
         return pl.ds(pl.multiple_of(g * width, width), width)
@@ -220,19 +345,21 @@
             inv = 1.0 / jnp.sum(e, axis=0, keepdims=True)
             pbuf[g, :, h * HEAD_SIZE:(h + 1) * HEAD_SIZE] = (e * inv).astype(BF16)
         dv = dot(pbuf[g], stack(do, g))
-        dv_own[:, lanes(g, HEAD_SIZE)] = dv[0:TILE]
-        for d in range(1, reach + 1):
-            dv_send[g, d - 1] = dv[d * TILE:(d + 1) * TILE].astype(BF16)
-
-            @pl.when(me >= d)
-            def _():
-                backward(dv_send, dv_recv, g, d, dv_s, dv_r).start()
+        send_terms(dv_buf, dv_s, dv_r, g, dv)
+
+        @pl.when(jnp.logical_and(g >= 1, me >= 2))
+        def _():
+            finish_terms(dv_buf, dv_s, dv_r, g - 1)
         return carry
 
     lax.fori_loop(0, groups, first, 0)
 
+    @pl.when(me >= 2)
+    def _():
+        finish_terms(dv_buf, dv_s, dv_r, groups - 1)
+    relay(fwin, f_s, f_r)
+
     loads[4].wait()
-    loads[5].wait()
     wait_arrivals(recv_a, a_s, a_r)
     per = max(1, 512 // piece)
     low_t = jnp.zeros((R, TILE), F32)
@@ -248,27 +375,14 @@
         ups.append(dot(jnp.where(hit, 1.0, 0.0).astype(BF16), recv_a[:, piece:piece + up_lanes]))
     up = jnp.concatenate(ups, axis=1)
     up_half = up.astype(BF16)
-    low = jnp.concatenate([low_t, jnp.zeros((TILE - R, TILE), F32)], axis=0).T.astype(BF16)
     up_tall = jnp.concatenate([up, jnp.zeros((TILE - R, kvw), F32)], axis=0).astype(BF16)
-    vwin[0] = (frozen[...].astype(F32) + ADAPTER_SCALE * dot(low, up_tall)).astype(BF16)
+    lwin[0] = low_half
     for d in range(1, reach + 1):
         @pl.when(me + d < n)
         def _():
-            forward(vwin, d, v_s, v_r).start()
-
-    def gather_back(own, send, recv, out, ss, rs):
-        for d in range(1, reach + 1):
-            @pl.when(me + d < n)
-            def _():
-                for g in range(groups):
-                    backward(send, recv, g, d, ss, rs).wait_recv()
-        for g in range(groups):
-            acc = own[:, g * HEAD_SIZE:(g + 1) * HEAD_SIZE]
-            for d in range(1, reach + 1):
-                acc = acc + recv[g, d - 1].astype(F32)
-            out[:, g * HEAD_SIZE:(g + 1) * HEAD_SIZE] = acc.astype(BF16)
-
-    gather_back(dv_own, dv_send, dv_recv, dv_ref, dv_s, dv_r)
+            low_copy(d).start()
+
+    gather_back(dv_buf, dv_ref, dv_s, dv_r)
     dv = dv_ref[...]
     grad_t = (ADAPTER_SCALE * dot_nt(up_half, dv)).astype(BF16)
     up_grad = ADAPTER_SCALE * dot(low_half, dv)
@@ -286,10 +400,15 @@
 
     recv_g[rows(me), :] = send_g[rows(me), :]
 
+    settle(fwin, f_s, f_r)
     for d in range(1, reach + 1):
         @pl.when(me >= d)
         def _():
-            forward(vwin, d, v_s, v_r).wait_recv()
+            low_copy(d).wait_recv()
+
+    for d in range(reach + 1):
+        low = jnp.concatenate([lwin[d].astype(F32), jnp.zeros((TILE - R, TILE), F32)], axis=0).T
+        vwin[d] = (fwin[d].astype(F32) + ADAPTER_SCALE * dot(low.astype(BF16), up_tall)).astype(BF16)
 
     def dq_out(g):
         return pltpu.make_async_copy(dqv.at[g], dq_hbm.at[:, lanes(g, gw)], dq_sem.at[g])
@@ -306,13 +425,11 @@
             dsbuf[:, at] = (p * ((dp - delta) * scale)).astype(BF16)
         ds = dsbuf[...]
         dk = dot(ds, stack(q, g))
-        dk_own[:, lanes(g, HEAD_SIZE)] = dk[0:TILE]
-        for d in range(1, reach + 1):
-            dk_send[g, d - 1] = dk[d * TILE:(d + 1) * TILE].astype(BF16)
-
-            @pl.when(me >= d)
-            def _():
-                backward(dk_send, dk_recv, g, d, dk_s, dk_r).start()
+        send_terms(dk_buf, dk_s, dk_r, g, dk)
+
+        @pl.when(jnp.logical_and(g >= 1, me >= 2))
+        def _():
+            finish_terms(dk_buf, dk_s, dk_r, g - 1)
         dq_t = dot(kg.astype(F32).T.astype(BF16), dsbuf[...])
         for h in range(heads):
             at = slice(h * HEAD_SIZE, (h + 1) * HEAD_SIZE)
@@ -321,6 +438,10 @@
         return carry
 
     lax.fori_loop(0, groups, second, 0)
+
+    @pl.when(me >= 2)
+    def _():
+        finish_terms(dk_buf, dk_s, dk_r, groups - 1)
 
     wait_arrivals(recv_g, g_s, g_r)
     line = lax.broadcasted_iota(jnp.int32, (16, n * R), 0)
@@ -332,24 +453,33 @@
             gu_ref[b * 16:(b + 1) * 16, k * up_lanes:(k + 1) * up_lanes] = dot(
                 jnp.where(hit, 1.0, 0.0).astype(BF16), recv_g[:, piece:piece + up_lanes]
             )
-    gather_back(dk_own, dk_send, dk_recv, dk_ref, dk_s, dk_r)
+    gather_back(dk_buf, dk_ref, dk_s, dk_r)
 
     for g in range(groups):
         dq_out(g).wait()
     for d in range(1, reach + 1):
         @pl.when(me + d < n)
         def _():
-            forward(kwin, d, k_s, k_r).wait_send()
-            forward(vwin, d, v_s, v_r).wait_send()
-
-        @pl.when(me >= d)
-        def _():
-            for g in range(groups):
-                backward(dv_send, dv_recv, g, d, dv_s, dv_r).wait_send()
-                backward(dk_send, dk_recv, g, d, dk_s, dk_r).wait_send()
-
+            low_copy(d).wait_send()
+    spread_sent(kwin, k_s, k_r)
+    spread_sent(fwin, f_s, f_r)
+    terms_sent(dv_buf, dv_s, dv_r)
+    terms_sent(dk_buf, dk_s, dk_r)
     wait_sends(send_a, recv_a, a_s, a_r)
     wait_sends(send_g, recv_g, g_s, g_r)
+
+
+def flush(*refs):
+    ins, outs, held, sems = refs[0:5], refs[5:10], refs[10:15], refs[15]
+    loads = [pltpu.make_async_copy(ins[i], held[i], sems.at[i]) for i in range(5)]
+    stores = [pltpu.make_async_copy(held[i], outs[i], sems.at[5 + i]) for i in range(5)]
+    for load in loads:
+        load.start()
+    for load, store in zip(loads, stores):
+        load.wait()
+        store.start()
+    for store in stores:
+        store.wait()
 
 
 def per_device(
@@ -367,13 +497,13 @@
     window = (reach + 1) * row_count
     wide = piece + min(up_piece, 128)
     vmem = pl.BlockSpec(memory_space=pltpu.VMEM)
-    smem = pl.BlockSpec(memory_space=pltpu.SMEM)
-    hbm = pl.BlockSpec(memory_space=pl.ANY)
+    hbm = pl.BlockSpec(memory_space=pltpu.HBM)
+    anywhere = pl.BlockSpec(memory_space=pl.ANY)
     sem = pltpu.SemaphoreType.DMA
-    terms = pltpu.VMEM((groups, reach, row_count, HEAD_SIZE), BF16)
-    own = pltpu.VMEM((row_count, kvw), F32)
+    block = (groups, row_count, HEAD_SIZE)
+    terms = [pltpu.VMEM(block, F32)] * 2 + [pltpu.VMEM(block, BF16)] * 6
     a2a = pltpu.VMEM((n * R, wide), BF16)
-    d_queries, d_keys, d_values, grad_down, grad_up = pl.pallas_call(
+    results = pl.pallas_call(
         functools.partial(kernel, n, reach),
         out_shape=(
             jax.ShapeDtypeStruct((row_count, qw), BF16),
@@ -382,15 +512,19 @@
             jax.ShapeDtypeStruct((adapters, R, piece), F32),
             jax.ShapeDtypeStruct((adapters, up_piece), F32),
         ),
-        in_specs=[smem, smem, hbm, hbm, hbm, hbm, hbm, hbm, vmem],
-        out_specs=(hbm, vmem, vmem, vmem, vmem),
+        in_specs=[hbm] * 9,
+        out_specs=(anywhere, vmem, vmem, vmem, vmem),
         scratch_shapes=[
+            pltpu.SMEM(seg_tiles.shape, jnp.int32),
+            pltpu.SMEM(seg_tenant.shape, jnp.int32),
+            pltpu.VMEM((adapters, up_piece), BF16),
             pltpu.VMEM((row_count, d_model), BF16),
             pltpu.VMEM((row_count, qw), BF16),
             pltpu.VMEM((row_count, qw), BF16),
-            pltpu.VMEM((row_count, kvw), BF16),
             pltpu.VMEM((adapters, R, piece), BF16),
             pltpu.VMEM((reach + 1, row_count, kvw), BF16),
+            pltpu.VMEM((reach + 1, row_count, kvw), BF16),
+            pltpu.VMEM((reach + 1, R, row_count), BF16),
             pltpu.VMEM((reach + 1, row_count, kvw), BF16),
             pltpu.VMEM((adapters, up_piece), F32),
             a2a,
@@ -399,27 +533,35 @@
             pltpu.VMEM((window, gw), BF16),
             pltpu.VMEM((groups, row_count, gw), BF16),
             pltpu.VMEM((TILE, TILE), F32),
-            own, terms, terms,
-            own, terms, terms,
+            terms, terms,
             a2a,
             a2a,
             pltpu.VMEM((adapters * R, n * R), BF16),
             pltpu.SMEM((n,), jnp.int32),
-            sem((6,)),
+            sem((9,)),
             sem((groups,)),
-            sem((reach,)), sem((reach,)), sem((reach,)), sem((reach,)),
+            sem((4,)), sem((3,)), sem((4,)), sem((3,)),
+            sem((3,)), sem((3,)),
             sem((n,)), sem((n,)),
-            sem((groups * reach,)), sem((groups * reach,)),
-            sem((groups * reach,)), sem((groups * reach,)),
+            sem((3, groups)), sem((3, groups)),
+            sem((3, groups)), sem((3, groups)),
             sem((n,)), sem((n,)),
         ],
         compiler_params=pltpu.CompilerParams(
-            collective_id=0, has_side_effects=True, vmem_limit_bytes=48 * 1024 * 1024
+            collective_id=0, has_side_effects=True, vmem_limit_bytes=64 * 1024 * 1024
         ),
     )(
         seg_tiles, seg_tenant, hidden_in, queries, keys, frozen_values, d_out,
         jnp.swapaxes(adapter_down, 1, 2), adapter_up,
     )
+    d_queries, d_keys, d_values, grad_down, grad_up = pl.pallas_call(
+        flush,
+        out_shape=tuple(jax.ShapeDtypeStruct(x.shape, x.dtype) for x in results),
+        in_specs=[anywhere] * 5,
+        out_specs=(hbm,) * 5,
+        scratch_shapes=[pltpu.VMEM(x.shape, x.dtype) for x in results] + [sem((10,))],
+        compiler_params=pltpu.CompilerParams(vmem_limit_bytes=64 * 1024 * 1024),
+    )(*results)
     return (d_queries, d_keys, d_values, jnp.swapaxes(grad_down, 1, 2), grad_up)
 
 

time: 62.7 us -> 43.7 us (0.70)
  local copies, waits for them, and re-layouts: 10.9 us -> 0 us
  Pallas kernels: 50.8 us -> 42.4 us
    unnamed x21 -> x0, local copies, waits for them, and re-layouts: 10.9 us -> none
    pallas_call x1, Pallas kernels: 50.8 us -> 39.9 us  [per_device(): pl.pallas_call(functools.partial(kernel, n, reach), out_shape=(jax.ShapeD...]
    pallas_call x0 -> x1, Pallas kernels: none -> 2.54 us  [per_device(): pl.pallas_call(flush, out_shape=tuple((jax.ShapeDtypeStruct(x.shape, x.dt...]
where the time goes in v2:
time: 43.7 us; the launch traced here: 43.1 us
  Pallas kernels  42.4 us (97%)
  between operations  0.64 us (1%)
    pallas_call x1, Pallas kernels, per_device(): pl.pallas_call(functools.partial(kernel, n, reach), out_shape=(jax.ShapeD...  39.9 us
    pallas_call x1, Pallas kernels, per_device(): pl.pallas_call(flush, out_shape=tuple((jax.ShapeDtypeStruct(x.shape, x.dt...  2.54 us

profile of v2, /device:TPU:1, one launch (start us, length us, event | category | flops | bytes accessed | tf_op | source)
XLA Modules:
  0.0 43.1 jit_solution(6494840326101039505)
XLA Ops:
  0.6 39.9 %shard_map.128 = (bf16[128,4096]{1,0:T(8,128)(2,1)}, bf16[128,512]{1,0:T(8,128)(2,1)}, bf16[128,512]{1,0:T(8,128)(2,1)}, f32[16,16,512]{2,1,0:T(8,128)}, f32[16,512]{1,0:T(8,128)}) custom-call(s32[8]{0:T(128)} %tiles_hbm.1, s32[8]{0:T(128)} %tenant_hbm.1, bf16[128,8192]{1,0:T(8,128)(2,1)} %hidden_hbm.1, bf16[128,4096]{1,0:T(8,128)(2,1)} %q_hbm.1, ...), custom_call_target="tpu_custom_call" | custom-call | tf_op jit(solution)/shard_map/pallas_call | solution.py:506
  40.5 2.5 %shard_map.129 = (bf16[128,4096]{1,0:T(8,128)(2,1)}, bf16[128,512]{1,0:T(8,128)(2,1)}, bf16[128,512]{1,0:T(8,128)(2,1)}, f32[16,16,512]{2,1,0:T(8,128)}, f32[16,512]{1,0:T(8,128)}) custom-call(bf16[128,4096]{1,0:T(8,128)(2,1)} %get-tuple-element.15.refs_0_, bf16[128,512]{1,0:T(8,128)(2,1)} %get-tuple-element.16.refs_1_, ...), custom_call_target="tpu_custom_call" | custom-call | tf_op jit(solution)/shard_map/pallas_call | solution.py:557

commit v3 on v2

--- a/solution.py
+++ b/solution.py
@@ -30,7 +30,7 @@
 def kernel(
     n, reach, tiles_hbm, tenant_hbm, hidden_hbm, q_hbm, keys_hbm, frozen_hbm, do_hbm, down_hbm, up_hbm,
     dq_hbm, dk_ref, dv_ref, gd_ref, gu_ref,
-    seg_tiles, seg_tenant, up_in, hidden, q, do, down, kwin, fwin, lwin, vwin, upf, send_a, recv_a, pbuf, dsbuf, dqv, tri,
+    seg_tiles, seg_tenant, up_in, hidden, q, do, down, kwin, fwin, lwin, vwin, upf, send_a, recv_a, pbuf, dqv, tri,
     dv_buf, dk_buf, send_g, recv_g, pick, ten,
     load_sem, dq_sem, k_s, k_r, f_s, f_r, l_s, l_r, a_s, a_r, dv_s, dv_r, dk_s, dk_r, g_s, g_r,
 ):
@@ -127,65 +127,71 @@
             device_id={"ctx": peer}, device_id_type=pl.DeviceIdType.MESH,
         )
 
-    def near(win, ss, rs):
-        return remote(win.at[0], win.at[1], ss.at[0], rs.at[0], partner)
-
-    def across(win, ss, rs):
-        return remote(win.at[0], win.at[2], ss.at[1], rs.at[1], lax.rem(me + 2, n))
-
-    def far(win, ss, rs):
-        return remote(win.at[0], win.at[3], ss.at[2], rs.at[2], lax.rem(me + 3, n))
-
-    def pass_on(win, ss, rs):
+    def lanes(g, width):
+        return pl.ds(pl.multiple_of(g * width, width), width)
+
+    def head(win, at, g):
+        return win.at[at, :, lanes(g, HEAD_SIZE)]
+
+    def near(win, ss, rs, g):
+        return remote(head(win, 0, g), head(win, 1, g), ss.at[0, g], rs.at[0, g], partner)
+
+    def across(win, ss, rs, g):
+        return remote(head(win, 0, g), head(win, 2, g), ss.at[1, g], rs.at[1, g], lax.rem(me + 2, n))
+
+    def far(win, ss, rs, g):
+        return remote(head(win, 0, g), head(win, 3, g), ss.at[2, g], rs.at[2, g], lax.rem(me + 3, n))
+
+    def pass_on(win, ss, rs, g):
         at = 3 - 2 * odd
-        return remote(win.at[2], win.at[at], ss.at[3], rs.at[at - 1], partner)
+        return remote(head(win, 2, g), head(win, at, g), ss.at[3, g], rs.at[at - 1, g], partner)
 
     far_too = jnp.logical_and(odd == 1, me + 3 < n)
 
-    def spread(win, ss, rs):
+    def spread(win, ss, rs, g):
         @pl.when(me + 2 < n)
         def _():
-            across(win, ss, rs).start()
+            across(win, ss, rs, g).start()
 
         @pl.when(far_too)
         def _():
-            far(win, ss, rs).start()
+            far(win, ss, rs, g).start()
 
         @pl.when(odd == 0)
         def _():
-            near(win, ss, rs).start()
-
-    def relay(win, ss, rs):
+            near(win, ss, rs, g).start()
+
+    def relay(win, ss, rs, g):
         @pl.when(me >= 2)
         def _():
-            across(win, ss, rs).wait_recv()
-            pass_on(win, ss, rs).start()
-
-    def settle(win, ss, rs):
+            across(win, ss, rs, g).wait_recv()
+            pass_on(win, ss, rs, g).start()
+
+    def settle(win, ss, rs, g):
         @pl.when(me >= 1)
         def _():
-            near(win, ss, rs).wait_recv()
+            near(win, ss, rs, g).wait_recv()
 
         @pl.when(me >= 3)
         def _():
-            far(win, ss, rs).wait_recv()
-
-    def spread_sent(win, ss, rs):
+            far(win, ss, rs, g).wait_recv()
+
+    def spread_sent(win, ss, rs, g):
         @pl.when(me + 2 < n)
         def _():
-            across(win, ss, rs).wait_send()
+            across(win, ss, rs, g).wait_send()
 
         @pl.when(far_too)
         def _():
-            far(win, ss, rs).wait_send()
+            far(win, ss, rs, g).wait_send()
 
         @pl.when(odd == 0)
         def _():
-            near(win, ss, rs).wait_send()
+            near(win, ss, rs, g).wait_send()
 
         @pl.when(me >= 2)
         def _():
-            pass_on(win, ss, rs).wait_send()
+            pass_on(win, ss, rs, g).wait_send()
 
     def meet(buf, ss, rs, g):
         return remote(buf[2].at[g], buf[5].at[g], ss.at[0, g], rs.at[0, g], partner)
@@ -285,26 +291,26 @@
             tail = jnp.where(row_id == k, row[:, k * up_lanes:(k + 1) * up_lanes], tail)
         return down[tenant], tail.astype(BF16)
 
-    loads[0].wait()
-    loads[1].wait()
-    pl.semaphore_wait(barrier, n - 1)
-    spread(kwin, k_s, k_r)
-
-    def give(i, carry):
+    def prepare(i, carry):
         peer = lax.rem(me + i, n)
         mat, tail = factors(peer)
         send_a[rows(peer), 0:piece] = mat
         send_a[rows(peer), piece:piece + up_lanes] = tail
-        scatter(send_a, recv_a, peer, a_s, a_r).start()
         return carry
 
-    lax.fori_loop(1, n, give, 0)
+    def give(i, carry):
+        scatter(send_a, recv_a, lax.rem(me + i, n), a_s, a_r).start()
+        return carry
+
+    loads[1].wait()
+    lax.fori_loop(1, n, prepare, 0)
+    loads[0].wait()
+    pl.semaphore_wait(barrier, n - 1)
+    for g in range(groups):
+        spread(kwin, k_s, k_r, g)
     mat, tail = factors(me)
     recv_a[rows(me), 0:piece] = mat
     recv_a[rows(me), piece:piece + up_lanes] = tail
-    loads[5].wait()
-    spread(fwin, f_s, f_r)
-    relay(kwin, k_s, k_r)
 
     col = lax.broadcasted_iota(jnp.int32, (1, n * R), 1)
     col_tile = jnp.right_shift(col, 4)
@@ -322,16 +328,19 @@
 
     loads[2].wait()
     loads[3].wait()
-    settle(kwin, k_s, k_r)
-
-    def lanes(g, width):
-        return pl.ds(pl.multiple_of(g * width, width), width)
+    for g in range(2):
+        relay(kwin, k_s, k_r, g)
+    lax.fori_loop(1, n, give, 0)
+    loads[5].wait()
+    for g in range(groups):
+        spread(fwin, f_s, f_r, g)
 
     def stack(ref, g):
         part = ref[:, lanes(g, gw)]
         return jnp.concatenate([part[:, h * HEAD_SIZE:(h + 1) * HEAD_SIZE] for h in range(heads)], axis=0)
 
     def first(g, carry):
+        settle(kwin, k_s, k_r, g)
         kg = kwin[:, :, lanes(g, HEAD_SIZE)].reshape(window, HEAD_SIZE)
         qg = q[:, lanes(g, gw)]
         for h in range(heads):
@@ -347,6 +356,10 @@
         dv = dot(pbuf[g], stack(do, g))
         send_terms(dv_buf, dv_s, dv_r, g, dv)
 
+        @pl.when(g + 2 < groups)
+        def _():
+            relay(kwin, k_s, k_r, jnp.minimum(g + 2, groups - 1))
+
         @pl.when(jnp.logical_and(g >= 1, me >= 2))
         def _():
             finish_terms(dv_buf, dv_s, dv_r, g - 1)
@@ -357,7 +370,8 @@
     @pl.when(me >= 2)
     def _():
         finish_terms(dv_buf, dv_s, dv_r, groups - 1)
-    relay(fwin, f_s, f_r)
+    for g in range(groups):
+        relay(fwin, f_s, f_r, g)
 
     loads[4].wait()
     wait_arrivals(recv_a, a_s, a_r)
@@ -400,7 +414,8 @@
 
     recv_g[rows(me), :] = send_g[rows(me), :]
 
-    settle(fwin, f_s, f_r)
+    for g in range(groups):
+        settle(fwin, f_s, f_r, g)
     for d in range(1, reach + 1):
         @pl.when(me >= d)
         def _():
@@ -414,7 +429,6 @@
         return pltpu.make_async_copy(dqv.at[g], dq_hbm.at[:, lanes(g, gw)], dq_sem.at[g])
 
     def second(g, carry):
-        kg = kwin[:, :, lanes(g, HEAD_SIZE)].reshape(window, HEAD_SIZE)
         vg = vwin[:, :, lanes(g, HEAD_SIZE)].reshape(window, HEAD_SIZE)
         dog = do[:, lanes(g, gw)]
         for h in range(heads):
@@ -422,26 +436,31 @@
             dp = dot_nt(vg, dog[:, at])
             p = pbuf[g, :, at].astype(F32)
             delta = jnp.sum(p * dp, axis=0, keepdims=True)
-            dsbuf[:, at] = (p * ((dp - delta) * scale)).astype(BF16)
-        ds = dsbuf[...]
-        dk = dot(ds, stack(q, g))
+            pbuf[g, :, at] = (p * ((dp - delta) * scale)).astype(BF16)
+        dk = dot(pbuf[g], stack(q, g))
         send_terms(dk_buf, dk_s, dk_r, g, dk)
 
         @pl.when(jnp.logical_and(g >= 1, me >= 2))
         def _():
             finish_terms(dk_buf, dk_s, dk_r, g - 1)
-        dq_t = dot(kg.astype(F32).T.astype(BF16), dsbuf[...])
+        return carry
+
+    lax.fori_loop(0, groups, second, 0)
+
+    @pl.when(me >= 2)
+    def _():
+        finish_terms(dk_buf, dk_s, dk_r, groups - 1)
+
+    def third(g, carry):
+        kg = kwin[:, :, lanes(g, HEAD_SIZE)].reshape(window, HEAD_SIZE)
+        dq_t = dot(kg.astype(F32).T.astype(BF16), pbuf[g])
         for h in range(heads):
             at = slice(h * HEAD_SIZE, (h + 1) * HEAD_SIZE)
             dqv[g, :, at] = dq_t[:, at].T.astype(BF16)
         dq_out(g).start()
         return carry
 
-    lax.fori_loop(0, groups, second, 0)
-
-    @pl.when(me >= 2)
-    def _():
-        finish_terms(dk_buf, dk_s, dk_r, groups - 1)
+    lax.fori_loop(0, groups, third, 0)
 
     wait_arrivals(recv_g, g_s, g_r)
     line = lax.broadcasted_iota(jnp.int32, (16, n * R), 0)
@@ -461,8 +480,9 @@
         @pl.when(me + d < n)
         def _():
             low_copy(d).wait_send()
-    spread_sent(kwin, k_s, k_r)
-    spread_sent(fwin, f_s, f_r)
+    for g in range(groups):
+        spread_sent(kwin, k_s, k_r, g)
+        spread_sent(fwin, f_s, f_r, g)
     terms_sent(dv_buf, dv_s, dv_r)
     terms_sent(dk_buf, dk_s, dk_r)
     wait_sends(send_a, recv_a, a_s, a_r)
@@ -530,7 +550,6 @@
             a2a,
             a2a,
             pltpu.VMEM((groups, window, gw), BF16),
-            pltpu.VMEM((window, gw), BF16),
             pltpu.VMEM((groups, row_count, gw), BF16),
             pltpu.VMEM((TILE, TILE), F32),
             terms, terms,
@@ -540,7 +559,7 @@
             pltpu.SMEM((n,), jnp.int32),
             sem((9,)),
             sem((groups,)),
-            sem((4,)), sem((3,)), sem((4,)), sem((3,)),
+            sem((4, groups)), sem((3, groups)), sem((4, groups)), sem((3, groups)),
             sem((3,)), sem((3,)),
             sem((n,)), sem((n,)),
             sem((3, groups)), sem((3, groups)),

time: 43.7 us -> 40.3 us (0.922)
  the two profiles are of different devices: /device:TPU:1 before, /device:TPU:15 now
where the time goes in v3:
time: 40.3 us; the launch traced here: 40.2 us
  Pallas kernels  39.5 us (98%)
  between operations  0.64 us (2%)
    pallas_call x1, Pallas kernels, per_device(): pl.pallas_call(functools.partial(kernel, n, reach), out_shape=(jax.ShapeD...  37 us
    pallas_call x1, Pallas kernels, per_device(): pl.pallas_call(flush, out_shape=tuple((jax.ShapeDtypeStruct(x.shape, x.dt...  2.54 us

profile of v3, /device:TPU:15, one launch (start us, length us, event | category | flops | bytes accessed | tf_op | source)
XLA Modules:
  0.0 40.2 jit_solution(2540747358289556813)
XLA Ops:
  0.6 37.0 %shard_map.128 = (bf16[128,4096]{1,0:T(8,128)(2,1)}, bf16[128,512]{1,0:T(8,128)(2,1)}, bf16[128,512]{1,0:T(8,128)(2,1)}, f32[16,16,512]{2,1,0:T(8,128)}, f32[16,512]{1,0:T(8,128)}) custom-call(s32[8]{0:T(128)} %tiles_hbm.1, s32[8]{0:T(128)} %tenant_hbm.1, bf16[128,8192]{1,0:T(8,128)(2,1)} %hidden_hbm.1, bf16[128,4096]{1,0:T(8,128)(2,1)} %q_hbm.1, ...), custom_call_target="tpu_custom_call" | custom-call | tf_op jit(solution)/shard_map/pallas_call | solution.py:526
  37.6 2.5 %shard_map.129 = (bf16[128,4096]{1,0:T(8,128)(2,1)}, bf16[128,512]{1,0:T(8,128)(2,1)}, bf16[128,512]{1,0:T(8,128)(2,1)}, f32[16,16,512]{2,1,0:T(8,128)}, f32[16,512]{1,0:T(8,128)}) custom-call(bf16[128,4096]{1,0:T(8,128)(2,1)} %get-tuple-element.15.refs_0_, bf16[128,512]{1,0:T(8,128)(2,1)} %get-tuple-element.16.refs_1_, ...), custom_call_target="tpu_custom_call" | custom-call | tf_op jit(solution)/shard_map/pallas_call | solution.py:576

commit v4 on v3

--- a/solution.py
+++ b/solution.py
@@ -29,7 +29,8 @@
 
 def kernel(
     n, reach, tiles_hbm, tenant_hbm, hidden_hbm, q_hbm, keys_hbm, frozen_hbm, do_hbm, down_hbm, up_hbm,
-    dq_hbm, dk_ref, dv_ref, gd_ref, gu_ref,
+    dq_hbm, dk_hbm, dv_hbm, gd_hbm, gu_hbm,
+    dk_ref, dv_ref, gd_ref, gu_ref, out_sem,
     seg_tiles, seg_tenant, up_in, hidden, q, do, down, kwin, fwin, lwin, vwin, upf, send_a, recv_a, pbuf, dqv, tri,
     dv_buf, dk_buf, send_g, recv_g, pick, ten,
     load_sem, dq_sem, k_s, k_r, f_s, f_r, l_s, l_r, a_s, a_r, dv_s, dv_r, dk_s, dk_r, g_s, g_r,
@@ -396,7 +397,12 @@
         def _():
             low_copy(d).start()
 
+    outs = [
+        pltpu.make_async_copy(a, b, out_sem.at[i])
+        for i, (a, b) in enumerate(((dv_ref, dv_hbm), (gd_ref, gd_hbm), (gu_ref, gu_hbm), (dk_ref, dk_hbm)))
+    ]
     gather_back(dv_buf, dv_ref, dv_s, dv_r)
+    outs[0].start()
     dv = dv_ref[...]
     grad_t = (ADAPTER_SCALE * dot_nt(up_half, dv)).astype(BF16)
     up_grad = ADAPTER_SCALE * dot(low_half, dv)
@@ -472,7 +478,10 @@
             gu_ref[b * 16:(b + 1) * 16, k * up_lanes:(k + 1) * up_lanes] = dot(
                 jnp.where(hit, 1.0, 0.0).astype(BF16), recv_g[:, piece:piece + up_lanes]
             )
+    outs[1].start()
+    outs[2].start()
     gather_back(dk_buf, dk_ref, dk_s, dk_r)
+    outs[3].start()
 
     for g in range(groups):
         dq_out(g).wait()
@@ -487,6 +496,8 @@
     terms_sent(dk_buf, dk_s, dk_r)
     wait_sends(send_a, recv_a, a_s, a_r)
     wait_sends(send_g, recv_g, g_s, g_r)
+    for out in outs:
+        out.wait()
 
 
 def flush(*refs):
@@ -516,7 +527,6 @@
     gw = qw // groups
     window = (reach + 1) * row_count
     wide = piece + min(up_piece, 128)
-    vmem = pl.BlockSpec(memory_space=pltpu.VMEM)
     hbm = pl.BlockSpec(memory_space=pltpu.HBM)
     anywhere = pl.BlockSpec(memory_space=pl.ANY)
     sem = pltpu.SemaphoreType.DMA
@@ -533,8 +543,13 @@
             jax.ShapeDtypeStruct((adapters, up_piece), F32),
         ),
         in_specs=[hbm] * 9,
-        out_specs=(anywhere, vmem, vmem, vmem, vmem),
+        out_specs=(hbm,) * 5,
         scratch_shapes=[
+            pltpu.VMEM((row_count, kvw), BF16),
+            pltpu.VMEM((row_count, kvw), BF16),
+            pltpu.VMEM((adapters, R, piece), F32),
+            pltpu.VMEM((adapters, up_piece), F32),
+            sem((4,)),
             pltpu.SMEM(seg_tiles.shape, jnp.int32),
             pltpu.SMEM(seg_tenant.shape, jnp.int32),
             pltpu.VMEM((adapters, up_piece), BF16),

time: 40.3 us -> 39.7 us (0.985)
  the two profiles are of different devices: /device:TPU:15 before, /device:TPU:11 now
where the time goes in v4:
time: 39.7 us; the launch traced here: 39.6 us
  Pallas kernels  38.9 us (98%)
  between operations  0.64 us (2%)
    pallas_call x1, Pallas kernels, per_device(): pl.pallas_call(functools.partial(kernel, n, reach), out_shape=(jax.ShapeD...  36.4 us
    pallas_call x1, Pallas kernels, per_device(): pl.pallas_call(flush, out_shape=tuple((jax.ShapeDtypeStruct(x.shape, x.dt...  2.54 us

profile of v4, /device:TPU:11, one launch (start us, length us, event | category | flops | bytes accessed | tf_op | source)
XLA Modules:
  0.0 39.6 jit_solution(1752933406598899837)
XLA Ops:
  0.6 36.4 %shard_map.128 = (bf16[128,4096]{1,0:T(8,128)(2,1)}, bf16[128,512]{1,0:T(8,128)(2,1)}, bf16[128,512]{1,0:T(8,128)(2,1)}, f32[16,16,512]{2,1,0:T(8,128)}, f32[16,512]{1,0:T(8,128)}) custom-call(s32[8]{0:T(128)} %tiles_hbm.1, s32[8]{0:T(128)} %tenant_hbm.1, bf16[128,8192]{1,0:T(8,128)(2,1)} %hidden_hbm.1, bf16[128,4096]{1,0:T(8,128)(2,1)} %q_hbm.1, ...), custom_call_target="tpu_custom_call" | custom-call | tf_op jit(solution)/shard_map/pallas_call | solution.py:536
  37.0 2.5 %shard_map.129 = (bf16[128,4096]{1,0:T(8,128)(2,1)}, bf16[128,512]{1,0:T(8,128)(2,1)}, bf16[128,512]{1,0:T(8,128)(2,1)}, f32[16,16,512]{2,1,0:T(8,128)}, f32[16,512]{1,0:T(8,128)}) custom-call(bf16[128,4096]{1,0:T(8,128)(2,1)} %get-tuple-element.15.refs_0_, bf16[128,512]{1,0:T(8,128)(2,1)} %get-tuple-element.16.refs_1_, ...), custom_call_target="tpu_custom_call" | custom-call | tf_op jit(solution)/shard_map/pallas_call | solution.py:591
